TPU v7x, 256 devices: a whole 4x4x8 slice. The times are simulated.
256 devices in a mesh: seq: 32 (over y, x, core), head: 8 (over z).
Axes of the slice: x: 4, y: 4, z: 8, core: 2. Of those that a mesh axis runs over, the one named last changes fastest.
Arguments:
- queries: bfloat16 [32, 128, 16384], P('seq', None, 'head'), parts along dimension 2
- cache_keys: bfloat16 [262144, 1024], P('seq', 'head'), parts along dimension 1
- cache_values: bfloat16 [262144, 1024], P('seq', 'head'), parts along dimension 1
- lengths: int32 [32], replicated, may hold values from 1 to 8192, as said below
- span_owner: int32 [1], replicated, may hold values from 0 to 31
Outputs:
- attended: bfloat16 [32, 128, 16384], P('seq', None, 'head'), parts along dimension 2
There are 8 independent parts, one for each index of `head`. A program takes and returns all parts, laid end to end along the dimension named above; an argument that names none is the same for every part. Nothing has to cross between parts.
Inputs may be any that keep to these rules, and one draw needn't show every extreme that they name: `lengths`: every shard but the last holds 8192 valid positions.
All inputs are finite; a program needn't handle non-finite values.
Results may differ from a plain program's by a relative error of at most 0.0019.
Values may be sent and summed in bfloat16 or wider, within the bound.
No kernel may reach another device: no remote copies, remote signals or barrier semaphores. Data moves between devices by JAX's collectives and lax.ppermute only.
A program may use at most 128 MiB of HBM per device.

v0:
```python
import functools
import math

import jax
import jax.numpy as jnp
from jax import lax
from jax.experimental import pallas as pl
from jax.experimental.pallas import tpu as pltpu
from jax.sharding import PartitionSpec as P

AXIS = "seq"
CHIPS = 16
HEAD = 128
PIECE = 64
TAIL = 8
ROWS = PIECE + TAIL
VROWS = HEAD + 16
BLOCK = 512
STEP = 512
BF16 = jnp.bfloat16
F32 = jnp.float32
LOG2_SCALE = math.log2(math.e) / math.sqrt(HEAD)
NT = (((1,), (1,)), ((), ()))

SWAP = [(i, i ^ 1) for i in range(2 * CHIPS)]
PLANE = [[2 * chip + core for chip in range(CHIPS)] for core in range(2)]


def vmem(limit):
    return pltpu.CompilerParams(vmem_limit_bytes=limit << 20)


def exchange(pieces):
    return lax.all_to_all(pieces, AXIS, 0, 0, axis_index_groups=PLANE, tiled=True)


def prepare_kernel(len_ref, k_ref, v_ref, kept_ref, turned_ref):
    size = v_ref.shape[0]
    kept_ref[...] = k_ref[...]
    lanes = lax.broadcasted_iota(jnp.int32, (HEAD, HEAD), 1)
    eye = (lanes == lax.broadcasted_iota(jnp.int32, (HEAD, HEAD), 0)).astype(BF16)
    turned = lax.dot_general(eye, v_ref[...], NT, preferred_element_type=F32)
    column = pl.program_id(0) * size + lax.broadcasted_iota(jnp.int32, (1, size), 1)
    valid = column < len_ref[lax.axis_index(AXIS)]
    turned_ref[:HEAD, :] = jnp.where(valid, turned, 0.0).astype(BF16)
    turned_ref[HEAD:, :] = jnp.broadcast_to(jnp.where(valid, 1.0, 0.0), (16, size)).astype(BF16)


def prepare(lengths, keys, values):
    count = keys.shape[0]
    size = 2048
    rows = pl.BlockSpec((size, HEAD), lambda i, n: (i, 0))
    return pl.pallas_call(
        prepare_kernel,
        out_shape=(
            jax.ShapeDtypeStruct(keys.shape, BF16),
            jax.ShapeDtypeStruct((VROWS, count), BF16),
        ),
        grid_spec=pltpu.PrefetchScalarGridSpec(
            num_scalar_prefetch=1,
            grid=(count // size,),
            in_specs=[rows, rows],
            out_specs=(rows, pl.BlockSpec((VROWS, size), lambda i, n: (0, i))),
        ),
        compiler_params=vmem(16),
        cost_estimate=pl.CostEstimate(
            flops=4 * count * HEAD * HEAD, bytes_accessed=8 * count * HEAD, transcendentals=0
        ),
        name="prepare",
    )(lengths, keys, values)


def attention_kernel(q_ref, k_ref, v_ref, o_ref, acc_ref):
    q = q_ref[...]

    def write(out, sums, top):
        row = lax.broadcasted_iota(jnp.int32, (TAIL, HEAD), 0)
        for head in range(BLOCK // HEAD):
            lanes = slice(head * HEAD, (head + 1) * HEAD)
            tail = jnp.where(row < TAIL // 2, sums[:, lanes], top[:, lanes])
            for part in range(2):
                o_ref[2 * head + part, :PIECE, :] = out[part * PIECE : (part + 1) * PIECE, lanes]
                o_ref[2 * head + part, PIECE:, :] = tail

    scores = lax.dot_general(k_ref[...], q, NT, preferred_element_type=F32)
    weights = jnp.exp2(scores * LOG2_SCALE).astype(BF16)
    total = jnp.dot(v_ref[...], weights, preferred_element_type=F32)
    sums = total[HEAD : HEAD + 1, :]
    write(total[:HEAD], sums, jnp.zeros_like(sums))
    good = (sums >= 1.0) & (sums <= 2.0**20)
    bad = jnp.max(jnp.where(jnp.abs(total[:HEAD]) < 3e38, 0.0, 1.0), axis=0, keepdims=True)
    fine = jnp.max(jnp.where(good, bad, 1.0)) < 0.5

    @pl.when(jnp.logical_not(fine))
    def _():
        acc_ref[...] = jnp.zeros_like(acc_ref)
        valid_len = jnp.sum(v_ref[HEAD : HEAD + 1, :].astype(F32)).astype(jnp.int32)

        def body(i, top):
            start = pl.multiple_of(i * STEP, STEP)
            s = lax.dot_general(k_ref[pl.ds(start, STEP), :], q, NT, preferred_element_type=F32)
            row = start + lax.broadcasted_iota(jnp.int32, (STEP, 1), 0)
            s = jnp.where(row < valid_len, s * LOG2_SCALE, -jnp.inf)
            new_top = jnp.maximum(top, jnp.max(s, axis=0, keepdims=True))
            w = jnp.exp2(s - new_top).astype(BF16)
            part = jnp.dot(v_ref[:, pl.ds(start, STEP)], w, preferred_element_type=F32)
            acc_ref[...] = acc_ref[...] * jnp.exp2(top - new_top) + part
            return new_top

        start_top = jnp.full((1, BLOCK), -jnp.inf, F32)
        top = lax.fori_loop(0, k_ref.shape[0] // STEP, body, start_top)
        write(acc_ref[:HEAD, :], acc_ref[HEAD : HEAD + 1, :], top)


def attention(rows, keys, values, first, blocks):
    pieces = 2 * BLOCK // HEAD
    return pl.pallas_call(
        attention_kernel,
        out_shape=jax.ShapeDtypeStruct((blocks * pieces, ROWS, HEAD), F32),
        grid=(blocks,),
        in_specs=[
            pl.BlockSpec((BLOCK, HEAD), lambda i: (i + first, 0)),
            pl.BlockSpec(keys.shape, lambda i: (0, 0)),
            pl.BlockSpec(values.shape, lambda i: (0, 0)),
        ],
        out_specs=pl.BlockSpec((pieces, ROWS, HEAD), lambda i: (i, 0, 0)),
        scratch_shapes=[pltpu.VMEM((VROWS, BLOCK), F32)],
        compiler_params=vmem(44),
        cost_estimate=pl.CostEstimate(
            flops=4 * blocks * BLOCK * keys.shape[0] * HEAD,
            bytes_accessed=4 * keys.shape[0] * HEAD,
            transcendentals=blocks * BLOCK * keys.shape[0],
        ),
        name="attention",
    )(rows, keys, values)


def merge_kernel(a_ref, b_ref, peer_ref, o_ref):
    first = a_ref.shape[0]

    def put(mine, start):
        stop = start + mine.shape[0]
        top_a = mine[:, ROWS - 1 :, :]
        top_b = peer_ref[start:stop, ROWS - 1 :, :]
        top = jnp.maximum(top_a, top_b)
        left = jnp.exp2(top_a - top)
        right = jnp.exp2(top_b - top)
        o_ref[start:stop, :PIECE, :] = (
            left * mine[:, :PIECE, :] + right * peer_ref[start:stop, :PIECE, :]
        )
        sums = left * mine[:, PIECE : PIECE + 1, :]
        sums += right * peer_ref[start:stop, PIECE : PIECE + 1, :]
        row = lax.broadcasted_iota(jnp.int32, (1, TAIL, HEAD), 1)
        o_ref[start:stop, PIECE:, :] = jnp.where(row < TAIL // 2, sums, top)

    put(a_ref, 0)
    put(b_ref, first)


def merge(a, b, peer):
    return pl.pallas_call(
        merge_kernel,
        out_shape=jax.ShapeDtypeStruct(peer.shape, F32),
        compiler_params=vmem(16),
        name="merge",
    )(a, b, peer)


def split_kernel(q_ref, keep_ref, send_ref):
    half = q_ref.shape[1] // 2

    def put(ref, start):
        for h in range(half // HEAD):
            block = q_ref[:, start + h * HEAD : start + (h + 1) * HEAD]
            ref[2 * h] = block[:PIECE]
            ref[2 * h + 1] = block[PIECE:]

    core = lax.axis_index(AXIS) % 2

    @pl.when(core == 0)
    def _():
        put(keep_ref, 0)
        put(send_ref, half)

    @pl.when(core == 1)
    def _():
        put(keep_ref, half)
        put(send_ref, 0)


def split(block):
    shape = jax.ShapeDtypeStruct((CHIPS, PIECE, HEAD), BF16)
    return pl.pallas_call(
        split_kernel,
        out_shape=(shape, shape),
        compiler_params=vmem(16),
        name="split",
    )(block)


def choose_kernel(owner_ref, a_ref, b_ref, o_ref):
    mine = owner_ref[0] % 2 == lax.axis_index(AXIS) % 2

    @pl.when(mine)
    def _():
        o_ref[...] = a_ref[...]

    @pl.when(jnp.logical_not(mine))
    def _():
        o_ref[...] = b_ref[...]


def choose(owner, a, b):
    return pl.pallas_call(
        choose_kernel,
        out_shape=jax.ShapeDtypeStruct(a.shape, a.dtype),
        in_specs=[
            pl.BlockSpec(memory_space=pltpu.SMEM),
            pl.BlockSpec(memory_space=pltpu.VMEM),
            pl.BlockSpec(memory_space=pltpu.VMEM),
        ],
        compiler_params=vmem(16),
        name="choose",
    )(owner, a, b)


def finish_kernel(r_ref, o_ref):
    tops = r_ref[:, ROWS - 1 :, :]
    scale = jnp.exp2(tops - jnp.max(tops, axis=0, keepdims=True))
    denom = jnp.sum(scale * r_ref[:, PIECE : PIECE + 1, :], axis=0)
    numer = jnp.sum(scale * r_ref[:, :PIECE, :], axis=0)
    result = (numer / denom).astype(BF16)
    o_ref[...] = jnp.broadcast_to(result[None], o_ref.shape)


def finish(received):
    return pl.pallas_call(
        finish_kernel,
        out_shape=jax.ShapeDtypeStruct((CHIPS, PIECE, HEAD), BF16),
        compiler_params=vmem(16),
        name="finish",
    )(received)


def place_kernel(owner_ref, a_ref, b_ref, o_ref):
    half = o_ref.shape[1] // 2

    me = lax.axis_index(AXIS)
    wanted = me == owner_ref[0]

    @pl.when(jnp.logical_not(wanted))
    def _():
        o_ref[...] = jnp.zeros_like(o_ref)

    def put(first, second):
        for i, ref in enumerate((first, second)):
            for h in range(half // HEAD):
                block = ref[h * HEAD : (h + 1) * HEAD, :]
                o_ref[:, i * half + h * HEAD : i * half + (h + 1) * HEAD] = block.T

    @pl.when(wanted & (me % 2 == 0))
    def _():
        put(a_ref, b_ref)

    @pl.when(wanted & (me % 2 == 1))
    def _():
        put(b_ref, a_ref)


def place(owner, own, other):
    return pl.pallas_call(
        place_kernel,
        out_shape=jax.ShapeDtypeStruct((HEAD, 2 * own.shape[0]), BF16),
        in_specs=[
            pl.BlockSpec(memory_space=pltpu.SMEM),
            pl.BlockSpec(memory_space=pltpu.VMEM),
            pl.BlockSpec(memory_space=pltpu.VMEM),
        ],
        compiler_params=vmem(16),
        name="place",
    )(owner, own, other)


def per_device(queries, cache_keys, cache_values, lengths, span_owner):
    block = queries[0]
    half = block.shape[1] // 2

    keep, send = split(block)
    received = lax.ppermute(send, AXIS, SWAP)
    mine = choose(span_owner, keep, received)
    lengths, mine = lax.optimization_barrier((lengths, mine))
    keys, values = prepare(lengths, cache_keys, cache_values)
    piece = lax.dynamic_index_in_dim(exchange(mine), span_owner[0] // 2, 0, False)
    piece, keys, values = lax.optimization_barrier((piece, keys, values))
    own = exchange(jnp.broadcast_to(piece[None], mine.shape))
    other = lax.ppermute(own, AXIS, SWAP).reshape(half, HEAD)
    own = own.reshape(half, HEAD)

    attend = functools.partial(attention, keys=keys, values=values)
    blocks = half // BLOCK
    part_a = attend(own, first=0, blocks=blocks // 2)
    part_a, other = lax.optimization_barrier((part_a, other))
    part_other = attend(other, first=0, blocks=blocks)
    part_peer = lax.ppermute(part_other, AXIS, SWAP)
    own, _ = lax.optimization_barrier((own, part_other))
    part_b = attend(own, first=blocks // 2, blocks=blocks - blocks // 2)
    result = finish(exchange(merge(part_a, part_b, part_peer)))
    result = exchange(result)
    result_other = lax.ppermute(result, AXIS, SWAP)
    out = place(span_owner, result.reshape(half, HEAD), result_other.reshape(half, HEAD))
    return out[None]


def solution(mesh):
    return jax.shard_map(
        per_device,
        mesh=mesh,
        in_specs=(P("seq", None, "head"), P("seq", "head"), P("seq", "head"), P(), P()),
        out_specs=P("seq", None, "head"),
        check_vma=False,
    )
```

profile of v0, /device:TPU:1, one launch (start us, length us, event | category | flops | bytes accessed | tf_op | source)
XLA Modules:
  0.0 92.1 jit_solution(12773915224016551189)
XLA Ops:
  0.0 1.0 %copy-done.2 = bf16[1,128,2048]{2,1,0:T(8,128)(2,1)S(1)} copy-done((bf16[1,128,2048]{2,1,0:T(8,128)(2,1)S(1)}, bf16[1,128,2048]{2,1,0:T(8,128)(2,1)}, u32[]{:S(2)}) %copy-start.2) | copy-done | bytes 524312
  1.1 3.3 %collective-permute-start = (bf16[16,64,128]{2,1,0:T(8,128)(2,1)S(1)}, bf16[16,64,128]{2,1,0:T(8,128)(2,1)S(1)}, u32[]{:S(2)}, u32[]{:S(2)}) collective-permute-start(bf16[16,64,128]{2,1,0:T(8,128)(2,1)S(1)} %get-tuple-element.18), channel_id=1, source_target_pairs={{0,8},{8,0},{16,24},{24,16},{32,40},{40,32},{48,56},{56,48},{64,72... | collective-permute-start | bytes 786440 | tf_op jit(solution)/shard_map/ppermute | solution.py:289
  5.1 0.5 collective-permute-done.b_ref
  5.6 0.7 choose.1
  6.4 5.0 %all-to-all-start = ((bf16[16,64,128]{2,1,0:T(8,128)(2,1)}), bf16[16,64,128]{2,1,0:T(8,128)(2,1)S(1)}, u32[]{:S(2)}, u32[]{:S(2)}) async-start(bf16[16,64,128]{2,1,0:T(8,128)(2,1)} %choose.1), calls=%async_computation | async-start | bytes 524288 | tf_op jit(solution)/shard_map/all_to_all | solution.py:34
  11.4 1.6 %copy-done = bf16[8192,128]{1,0:T(8,128)(2,1)S(1)} copy-done((bf16[8192,128]{1,0:T(8,128)(2,1)S(1)}, bf16[8192,128]{1,0:T(8,128)(2,1)}, u32[]{:S(2)}) %copy-start) | copy-done | bytes 2097176
  13.0 1.6 %copy-done.1 = bf16[8192,128]{1,0:T(8,128)(2,1)S(1)} copy-done((bf16[8192,128]{1,0:T(8,128)(2,1)S(1)}, bf16[8192,128]{1,0:T(8,128)(2,1)}, u32[]{:S(2)}) %copy-start.1) | copy-done | bytes 2097176
  14.6 0.7 copy-done.3
  15.3 2.1 %prepare.1 = (bf16[8192,128]{1,0:T(8,128)(2,1)S(1)}, bf16[144,8192]{1,0:T(8,128)(2,1)S(1)}) custom-call(s32[32]{0:T(128)S(1)} %copy-done.3, bf16[8192,128]{1,0:T(8,128)(2,1)S(1)} %copy-done, bf16[8192,128]{1,0:T(8,128)(2,1)S(1)} %copy-done.1), custom_call_target="tpu_custom_call" | custom-call | flops 536870912 | bytes 8388608 | tf_op jit(solution)/shard_map/prepare/pallas_call | solution.py:53
  17.3 1.3 %copy-done.4 = bf16[8192,128]{1,0:T(8,128)(2,1)} copy-done((bf16[8192,128]{1,0:T(8,128)(2,1)}, bf16[8192,128]{1,0:T(8,128)(2,1)S(1)}, u32[]{:S(2)}) %copy-start.4) | copy-done | bytes 2097176
  18.6 0.8 all-to-all-done
  19.5 13.2 %all_to_all.20 = bf16[16,64,128]{2,1,0:T(8,128)(2,1)S(1)} all-to-all(bf16[16,64,128]{2,1,0:T(8,128)(2,1)S(1)} %broadcast_in_dim.4), channel_id=1, replica_groups={{0,16,32,48,64,80,96,112,128,144,160,176,192,208,224,240},{8,24,40,56,7..., dimensions={0} | all-to-all | bytes 524288 | tf_op jit(solution)/shard_map/all_to_all | solution.py:34
  32.8 2.3 %collective-permute-start.1 = (bf16[16,64,128]{2,1,0:T(8,128)(2,1)S(1)}, bf16[16,64,128]{2,1,0:T(8,128)(2,1)S(1)}, u32[]{:S(2)}, u32[]{:S(2)}) collective-permute-start(bf16[16,64,128]{2,1,0:T(8,128)(2,1)S(1)} %all_to_all.20), channel_id=1, source_target_pairs={{0,8},{8,0},{16,24},{24,16},{32,40},{40,32},{48,56},{56,48},{64,72... | collective-permute-start | bytes 786440 | tf_op jit(solution)/shard_map/ppermute | solution.py:296
  35.0 1.6 %copy-done.5 = bf16[8192,128]{1,0:T(8,128)(2,1)S(1)} copy-done((bf16[8192,128]{1,0:T(8,128)(2,1)S(1)}, bf16[8192,128]{1,0:T(8,128)(2,1)}, u32[]{:S(2)}) %copy-start.5) | copy-done | bytes 2097176
  36.6 3.7 %attention.3.a_ref = f32[8,72,128]{2,1,0:T(8,128)S(1)} custom-call(bf16[1024,128]{1,0:T(8,128)(2,1)S(1)} %bitcast.15, bf16[8192,128]{1,0:T(8,128)(2,1)S(1)} %copy-done.5, bf16[144,8192]{1,0:T(8,128)(2,1)S(1)} %get-tuple-element.25.v_ref), custom_call_target="tpu_custom_call" | custom-call | flops 2147483648 | bytes 4194304 | tf_op jit(solution)/shard_map/attention/pallas_call | solution.py:117
  40.3 18.0 %attention.4 = f32[16,72,128]{2,1,0:T(8,128)S(1)} custom-call(bf16[1024,128]{1,0:T(8,128)(2,1)S(1)} %bitcast.18, bf16[8192,128]{1,0:T(8,128)(2,1)S(1)} %copy-done.5, bf16[144,8192]{1,0:T(8,128)(2,1)S(1)} %get-tuple-element.25.v_ref), custom_call_target="tpu_custom_call" | custom-call | flops 4294967296 | bytes 4194304 | tf_op jit(solution)/shard_map/attention/pallas_call | solution.py:117
  58.3 0.3 collective-permute-start.2
  58.6 3.7 %attention.5.b_ref = f32[8,72,128]{2,1,0:T(8,128)S(1)} custom-call(bf16[1024,128]{1,0:T(8,128)(2,1)S(1)} %bitcast.16, bf16[8192,128]{1,0:T(8,128)(2,1)S(1)} %copy-done.5, bf16[144,8192]{1,0:T(8,128)(2,1)S(1)} %get-tuple-element.25.v_ref), custom_call_target="tpu_custom_call" | custom-call | flops 2147483648 | bytes 4194304 | tf_op jit(solution)/shard_map/attention/pallas_call | solution.py:117
  62.3 0.1 merge.1
  62.4 13.9 %all_to_all.21.r_ref = f32[16,72,128]{2,1,0:T(8,128)S(1)} all-to-all(f32[16,72,128]{2,1,0:T(8,128)S(1)} %merge.1), channel_id=1, replica_groups={{0,16,32,48,64,80,96,112,128,144,160,176,192,208,224,240},{8,24,40,56,7..., dimensions={0} | all-to-all | bytes 1179648 | tf_op jit(solution)/shard_map/all_to_all | solution.py:34
  76.4 10.8 %all_to_all.22 = bf16[16,64,128]{2,1,0:T(8,128)(2,1)S(1)} all-to-all(bf16[16,64,128]{2,1,0:T(8,128)(2,1)S(1)} %finish.1), channel_id=1, replica_groups={{0,16,32,48,64,80,96,112,128,144,160,176,192,208,224,240},{8,24,40,56,7..., dimensions={0} | all-to-all | bytes 524288 | tf_op jit(solution)/shard_map/all_to_all | solution.py:34
  87.2 2.9 %collective-permute-start.3 = (bf16[16,64,128]{2,1,0:T(8,128)(2,1)S(1)}, bf16[16,64,128]{2,1,0:T(8,128)(2,1)S(1)}, u32[]{:S(2)}, u32[]{:S(2)}) collective-permute-start(bf16[16,64,128]{2,1,0:T(8,128)(2,1)S(1)} %all_to_all.22), channel_id=1, source_target_pairs={{0,8},{8,0},{16,24},{24,16},{32,40},{40,32},{48,56},{56,48},{64,72... | collective-permute-start | bytes 786440 | tf_op jit(solution)/shard_map/ppermute | solution.py:309
  90.1 1.2 %collective-permute-done.3 = bf16[16,64,128]{2,1,0:T(8,128)(2,1)S(1)} collective-permute-done((bf16[16,64,128]{2,1,0:T(8,128)(2,1)S(1)}, bf16[16,64,128]{2,1,0:T(8,128)(2,1)S(1)}, u32[]{:S(2)}, u32[]{:S(2)}) %collective-permute-start.3) | collective-permute-done | bytes 262176 | tf_op jit(solution)/shard_map/ppermute | solution.py:309
  91.3 0.8 place.1
  (12 shorter events, 0.2 us)
Async XLA Ops:
  0.0 1.0 %copy-start.2 = (bf16[1,128,2048]{2,1,0:T(8,128)(2,1)S(1)}, bf16[1,128,2048]{2,1,0:T(8,128)(2,1)}, u32[]{:S(2)}) copy-start(bf16[1,128,2048]{2,1,0:T(8,128)(2,1)} %param.5) | copy-start | bytes 1572868
  1.1 4.5 %collective-permute-start = (bf16[16,64,128]{2,1,0:T(8,128)(2,1)S(1)}, bf16[16,64,128]{2,1,0:T(8,128)(2,1)S(1)}, u32[]{:S(2)}, u32[]{:S(2)}) collective-permute-start(bf16[16,64,128]{2,1,0:T(8,128)(2,1)S(1)} %get-tuple-element.18), channel_id=1, source_target_pairs={{0,8},{8,0},{16,24},{24,16},{32,40},{40,32},{48,56},{56,48},{64,72... | collective-permute-start | bytes 786440 | tf_op jit(solution)/shard_map/ppermute | solution.py:289
  6.4 13.1 %all-to-all-start = ((bf16[16,64,128]{2,1,0:T(8,128)(2,1)}), bf16[16,64,128]{2,1,0:T(8,128)(2,1)S(1)}, u32[]{:S(2)}, u32[]{:S(2)}) async-start(bf16[16,64,128]{2,1,0:T(8,128)(2,1)} %choose.1), calls=%async_computation | async-start | bytes 524288 | tf_op jit(solution)/shard_map/all_to_all | solution.py:34
  11.4 1.6 %copy-start = (bf16[8192,128]{1,0:T(8,128)(2,1)S(1)}, bf16[8192,128]{1,0:T(8,128)(2,1)}, u32[]{:S(2)}) copy-start(bf16[8192,128]{1,0:T(8,128)(2,1)} %k_ref.1) | copy-start | bytes 6291460
  13.0 1.6 %copy-start.1 = (bf16[8192,128]{1,0:T(8,128)(2,1)S(1)}, bf16[8192,128]{1,0:T(8,128)(2,1)}, u32[]{:S(2)}) copy-start(bf16[8192,128]{1,0:T(8,128)(2,1)} %v_ref.1) | copy-start | bytes 6291460
  14.6 0.7 copy-start.3
  17.3 1.3 %copy-start.4 = (bf16[8192,128]{1,0:T(8,128)(2,1)}, bf16[8192,128]{1,0:T(8,128)(2,1)S(1)}, u32[]{:S(2)}) copy-start(bf16[8192,128]{1,0:T(8,128)(2,1)S(1)} %get-tuple-element.24.k_ref) | copy-start | bytes 6291460
  32.8 7.5 %collective-permute-start.1 = (bf16[16,64,128]{2,1,0:T(8,128)(2,1)S(1)}, bf16[16,64,128]{2,1,0:T(8,128)(2,1)S(1)}, u32[]{:S(2)}, u32[]{:S(2)}) collective-permute-start(bf16[16,64,128]{2,1,0:T(8,128)(2,1)S(1)} %all_to_all.20), channel_id=1, source_target_pairs={{0,8},{8,0},{16,24},{24,16},{32,40},{40,32},{48,56},{56,48},{64,72... | collective-permute-start | bytes 786440 | tf_op jit(solution)/shard_map/ppermute | solution.py:296
  35.0 1.6 %copy-start.5 = (bf16[8192,128]{1,0:T(8,128)(2,1)S(1)}, bf16[8192,128]{1,0:T(8,128)(2,1)}, u32[]{:S(2)}) copy-start(bf16[8192,128]{1,0:T(8,128)(2,1)} %copy-done.4) | copy-start | bytes 6291460
  58.3 4.0 %collective-permute-start.2 = (f32[16,72,128]{2,1,0:T(8,128)S(1)}, f32[16,72,128]{2,1,0:T(8,128)S(1)}, u32[]{:S(2)}, u32[]{:S(2)}) collective-permute-start(f32[16,72,128]{2,1,0:T(8,128)S(1)} %attention.4), channel_id=1, source_target_pairs={{0,8},{8,0},{16,24},{24,16},{32,40},{40,32},{48,56},{56,48},{64,72... | collective-permute-start | bytes 1769480 | tf_op jit(solution)/shard_map/ppermute | solution.py:304
  87.2 4.1 %collective-permute-start.3 = (bf16[16,64,128]{2,1,0:T(8,128)(2,1)S(1)}, bf16[16,64,128]{2,1,0:T(8,128)(2,1)S(1)}, u32[]{:S(2)}, u32[]{:S(2)}) collective-permute-start(bf16[16,64,128]{2,1,0:T(8,128)(2,1)S(1)} %all_to_all.22), channel_id=1, source_target_pairs={{0,8},{8,0},{16,24},{24,16},{32,40},{40,32},{48,56},{56,48},{64,72... | collective-permute-start | bytes 786440 | tf_op jit(solution)/shard_map/ppermute | solution.py:309
where the time goes:
time: 92.6 us; the launch traced here: 92.1 us
  blocking collectives  38 us (41%)
  Pallas kernels  29.2 us (32%)
  starting transfers between devices  13.8 us (15%)
  local copies, waits for them, and re-layouts  7.83 us (8%)
  waiting for transfers between devices  2.52 us (3%)
    all_to_all x3, blocking collectives, exchange(): lax.all_to_all(pieces, AXIS, 0, 0, axis_index_groups=PLANE, tiled=True)  38 us
    pallas_call x3, Pallas kernels, attention(): pl.pallas_call(attention_kernel, out_shape=jax.ShapeDtypeStruct((blocks *...  25.3 us
    unnamed x12, local copies, waits for them, and re-layouts  7.78 us
    all_to_all x1, starting transfers between devices, exchange(): lax.all_to_all(pieces, AXIS, 0, 0, axis_index_groups=PLANE, tiled=True)  5.02 us
    ppermute x1, starting transfers between devices, per_device(): received = lax.ppermute(send, AXIS, SWAP)  3.33 us
    ppermute x1, starting transfers between devices, per_device(): result_other = lax.ppermute(result, AXIS, SWAP)  2.91 us
    ppermute x1, starting transfers between devices, per_device(): other = lax.ppermute(own, AXIS, SWAP).reshape(half, HEAD)  2.25 us
    pallas_call x1, Pallas kernels, prepare(): pl.pallas_call(prepare_kernel, out_shape=(jax.ShapeDtypeStruct(keys.shape...  2.06 us
  transfers between devices with their start and end apart: 5, of which 3 were waited for; matrix products, arithmetic and copies ran while one was open for 0% of the time, Pallas kernels for 10%

commit v1 on v0

v1 whole, which is shorter than its diff:
```python
import functools
import math

import jax
import jax.numpy as jnp
from jax import lax
from jax.experimental import pallas as pl
from jax.experimental.pallas import tpu as pltpu
from jax.sharding import PartitionSpec as P

AXIS = "seq"
CHIPS = 16
HEAD = 128
PIECE = 64
TAIL = 8
ROWS = PIECE + TAIL
VROWS = HEAD + 16
COLUMNS = 4
BLOCK = 512
PIECES = 2 * BLOCK // HEAD
STEP = 512
CHUNKS = 4
BF16 = jnp.bfloat16
F32 = jnp.float32
LOG2_SCALE = math.log2(math.e) / math.sqrt(HEAD)
NT = (((1,), (1,)), ((), ()))

SWAP = [(i, i ^ 1) for i in range(2 * CHIPS)]
PLANE = [[2 * chip + core for chip in range(CHIPS)] for core in range(2)]


def device(y, x, core):
    return (y * COLUMNS + x % COLUMNS) * 2 + core


def partner(y, x, core):
    return device(y, x + (1 if (x + core) % 2 == 0 else -1), core)


EVERY = [(y, x, core) for y in range(COLUMNS) for x in range(COLUMNS) for core in range(2)]
PAIR = [(device(*place), partner(*place)) for place in EVERY]
CROSS = [(device(y, x, 1 - core), partner(y, x, core)) for y, x, core in EVERY]
TEAMS = [
    [device(y, x, core) for y in range(COLUMNS) for x in (side, side + 2)]
    for core in range(2)
    for side in range(2)
]


def member(chip):
    y, x = divmod(chip, COLUMNS)
    return x % 2, 2 * y + x // 2


def vmem(limit):
    return pltpu.CompilerParams(vmem_limit_bytes=limit << 20)


def exchange(pieces, groups):
    return lax.all_to_all(pieces, AXIS, 0, 0, axis_index_groups=groups, tiled=True)


def values_kernel(len_ref, v_ref, o_ref):
    size = v_ref.shape[0]
    lanes = lax.broadcasted_iota(jnp.int32, (HEAD, HEAD), 1)
    eye = (lanes == lax.broadcasted_iota(jnp.int32, (HEAD, HEAD), 0)).astype(BF16)
    turned = lax.dot_general(eye, v_ref[...], NT, preferred_element_type=F32)
    column = pl.program_id(0) * size + lax.broadcasted_iota(jnp.int32, (1, size), 1)
    valid = column < len_ref[lax.axis_index(AXIS)]
    o_ref[:HEAD, :] = jnp.where(valid, turned, 0.0).astype(BF16)
    o_ref[HEAD:, :] = jnp.broadcast_to(jnp.where(valid, 1.0, 0.0), (16, size)).astype(BF16)


def turned_values(lengths, values):
    keys = values.shape[0]
    size = 2048
    return pl.pallas_call(
        values_kernel,
        out_shape=jax.ShapeDtypeStruct((VROWS, keys), BF16),
        grid_spec=pltpu.PrefetchScalarGridSpec(
            num_scalar_prefetch=1,
            grid=(keys // size,),
            in_specs=[pl.BlockSpec((size, HEAD), lambda i, n: (i, 0))],
            out_specs=pl.BlockSpec((VROWS, size), lambda i, n: (0, i)),
        ),
        compiler_params=vmem(16),
        cost_estimate=pl.CostEstimate(
            flops=4 * keys * HEAD * HEAD, bytes_accessed=5 * keys * HEAD, transcendentals=0
        ),
        name="turn_values",
    )(lengths, values)


def write_block(o_ref, out, sums, top):
    row = lax.broadcasted_iota(jnp.int32, (TAIL, HEAD), 0)
    for head in range(BLOCK // HEAD):
        lanes = slice(head * HEAD, (head + 1) * HEAD)
        tail = jnp.where(row < TAIL // 2, sums[:, lanes], top[:, lanes])
        for part in range(2):
            o_ref[2 * head + part, :PIECE, :] = out[part * PIECE : (part + 1) * PIECE, lanes]
            o_ref[2 * head + part, PIECE:, :] = tail


def weigh(q, keys, values):
    scores = lax.dot_general(keys, q, NT, preferred_element_type=F32)
    weights = jnp.exp2(scores * LOG2_SCALE).astype(BF16)
    return jnp.dot(values, weights, preferred_element_type=F32)


def settle(total, q, k_ref, v_ref, o_ref, acc_ref):
    sums = total[HEAD : HEAD + 1, :]
    write_block(o_ref, total[:HEAD], sums, jnp.zeros_like(sums))
    good = (sums >= 1.0) & (sums <= 2.0**20)
    bad = jnp.max(jnp.where(jnp.abs(total[:HEAD]) < 3e38, 0.0, 1.0), axis=0, keepdims=True)
    fine = jnp.max(jnp.where(good, bad, 1.0)) < 0.5

    @pl.when(jnp.logical_not(fine))
    def _():
        acc_ref[...] = jnp.zeros_like(acc_ref)
        valid_len = jnp.sum(v_ref[HEAD : HEAD + 1, :].astype(F32)).astype(jnp.int32)

        def body(i, top):
            at = pl.multiple_of(i * STEP, STEP)
            s = lax.dot_general(k_ref[pl.ds(at, STEP), :], q, NT, preferred_element_type=F32)
            row = at + lax.broadcasted_iota(jnp.int32, (STEP, 1), 0)
            s = jnp.where(row < valid_len, s * LOG2_SCALE, -jnp.inf)
            new_top = jnp.maximum(top, jnp.max(s, axis=0, keepdims=True))
            w = jnp.exp2(s - new_top).astype(BF16)
            part = jnp.dot(v_ref[:, pl.ds(at, STEP)], w, preferred_element_type=F32)
            acc_ref[...] = acc_ref[...] * jnp.exp2(top - new_top) + part
            return new_top

        start_top = jnp.full((1, BLOCK), -jnp.inf, F32)
        top = lax.fori_loop(0, k_ref.shape[0] // STEP, body, start_top)
        write_block(o_ref, acc_ref[:HEAD, :], acc_ref[HEAD : HEAD + 1, :], top)


def attention_kernel(q_ref, k_ref, v_ref, o_ref, acc_ref):
    q = q_ref[...]
    settle(weigh(q, k_ref[...], v_ref[...]), q, k_ref, v_ref, o_ref, acc_ref)


def first_attention_kernel(q_ref, k_ref, v_ref, o_ref, kept_ref, acc_ref, sems):
    size = k_ref.shape[0] // CHUNKS
    spans = [slice(i * size, (i + 1) * size) for i in range(CHUNKS)]
    copies = [
        pltpu.make_async_copy(k_ref.at[span], kept_ref.at[span], sems.at[i])
        for i, span in enumerate(spans)
    ]
    for copy in copies:
        copy.start()
    q = q_ref[...]
    total = None
    for copy, span in zip(copies, spans):
        copy.wait()
        part = weigh(q, kept_ref[span, :], v_ref[:, span])
        total = part if total is None else total + part
    settle(total, q, kept_ref, v_ref, o_ref, acc_ref)


def attention(rows, keys, values, first=False):
    vmem_spec = pl.BlockSpec(memory_space=pltpu.VMEM)
    out = jax.ShapeDtypeStruct((PIECES, ROWS, HEAD), F32)
    scratch = [pltpu.VMEM((VROWS, BLOCK), F32)]
    return pl.pallas_call(
        first_attention_kernel if first else attention_kernel,
        out_shape=(out, jax.ShapeDtypeStruct(keys.shape, BF16)) if first else out,
        in_specs=[vmem_spec, pl.BlockSpec(memory_space=pltpu.HBM) if first else vmem_spec, vmem_spec],
        out_specs=(vmem_spec, vmem_spec) if first else vmem_spec,
        scratch_shapes=scratch + ([pltpu.SemaphoreType.DMA((CHUNKS,))] if first else []),
        compiler_params=vmem(44),
        cost_estimate=pl.CostEstimate(
            flops=BLOCK * keys.size // 2, bytes_accessed=keys.size, transcendentals=0
        ),
        name="attention",
    )(rows.reshape(BLOCK, HEAD), keys, values)


def merge_kernel(*refs):
    parts, o_ref = refs[:-1], refs[-1]
    tops = [ref[:, ROWS - 1 :, :] for ref in parts]
    top = functools.reduce(jnp.maximum, tops)
    scales = [jnp.exp2(t - top) for t in tops]
    sums = sum(w * ref[:, PIECE : PIECE + 1, :] for w, ref in zip(scales, parts))
    row = lax.broadcasted_iota(jnp.int32, (1, TAIL, HEAD), 1)
    o_ref[:, :PIECE, :] = sum(w * ref[:, :PIECE, :] for w, ref in zip(scales, parts))
    o_ref[:, PIECE:, :] = jnp.where(row < TAIL // 2, sums, top)


def merge(*parts):
    return pl.pallas_call(
        merge_kernel,
        out_shape=jax.ShapeDtypeStruct(parts[0].shape, F32),
        compiler_params=vmem(16),
        name="merge",
    )(*parts)


def split_kernel(q_ref, keep_ref, send_ref):
    half = q_ref.shape[1] // 2

    def put(ref, start):
        for chip in range(CHIPS):
            side, place = member(chip)
            head, part = divmod((1 - side) * PIECES + place, 2)
            column = start + head * HEAD
            ref[chip] = q_ref[part * PIECE : (part + 1) * PIECE, column : column + HEAD]

    core = lax.axis_index(AXIS) % 2

    @pl.when(core == 0)
    def _():
        put(keep_ref, 0)
        put(send_ref, half)

    @pl.when(core == 1)
    def _():
        put(keep_ref, half)
        put(send_ref, 0)


def split(block):
    shape = jax.ShapeDtypeStruct((CHIPS, PIECE, HEAD), BF16)
    return pl.pallas_call(
        split_kernel,
        out_shape=(shape, shape),
        compiler_params=vmem(16),
        name="split",
    )(block)


def choose_kernel(owner_ref, a_ref, b_ref, o_ref):
    mine = owner_ref[0] % 2 == lax.axis_index(AXIS) % 2

    @pl.when(mine)
    def _():
        o_ref[...] = a_ref[...]

    @pl.when(jnp.logical_not(mine))
    def _():
        o_ref[...] = b_ref[...]


def choose(owner, a, b):
    return pl.pallas_call(
        choose_kernel,
        out_shape=jax.ShapeDtypeStruct(a.shape, a.dtype),
        in_specs=[
            pl.BlockSpec(memory_space=pltpu.SMEM),
            pl.BlockSpec(memory_space=pltpu.VMEM),
            pl.BlockSpec(memory_space=pltpu.VMEM),
        ],
        compiler_params=vmem(16),
        name="choose",
    )(owner, a, b)


def finish_kernel(r_ref, o_ref):
    tops = r_ref[:, ROWS - 1 :, :]
    scale = jnp.exp2(tops - jnp.max(tops, axis=0, keepdims=True))
    denom = jnp.sum(scale * r_ref[:, PIECE : PIECE + 1, :], axis=0)
    numer = jnp.sum(scale * r_ref[:, :PIECE, :], axis=0)
    result = (numer / denom).astype(BF16)
    o_ref[...] = jnp.broadcast_to(result[None], o_ref.shape)


def finish(received):
    return pl.pallas_call(
        finish_kernel,
        out_shape=jax.ShapeDtypeStruct((CHIPS, PIECE, HEAD), BF16),
        compiler_params=vmem(16),
        name="finish",
    )(received)


def place_kernel(owner_ref, a_ref, b_ref, o_ref):
    half = o_ref.shape[1] // 2

    me = lax.axis_index(AXIS)
    wanted = me == owner_ref[0]

    @pl.when(jnp.logical_not(wanted))
    def _():
        o_ref[...] = jnp.zeros_like(o_ref)

    def put(first, second):
        for i, ref in enumerate((first, second)):
            for chip in range(0, CHIPS):
                side, spot = member(chip)
                if spot % 2 == 0:
                    head = (side * PIECES + spot) // 2
                    block = jnp.concatenate([ref[chip], ref[chip + 2]], axis=0)
                    o_ref[:, i * half + head * HEAD : i * half + (head + 1) * HEAD] = block.T

    @pl.when(wanted & (me % 2 == 0))
    def _():
        put(a_ref, b_ref)

    @pl.when(wanted & (me % 2 == 1))
    def _():
        put(b_ref, a_ref)


def place(owner, own, other):
    return pl.pallas_call(
        place_kernel,
        out_shape=jax.ShapeDtypeStruct((HEAD, 2 * CHIPS * PIECE), BF16),
        in_specs=[
            pl.BlockSpec(memory_space=pltpu.SMEM),
            pl.BlockSpec(memory_space=pltpu.VMEM),
            pl.BlockSpec(memory_space=pltpu.VMEM),
        ],
        compiler_params=vmem(16),
        name="place",
    )(owner, own, other)


def per_device(queries, cache_keys, cache_values, lengths, span_owner):
    keep, send = split(queries[0])
    mine = choose(span_owner, keep, lax.ppermute(send, AXIS, SWAP))
    lengths, mine = lax.optimization_barrier((lengths, mine))
    values = turned_values(lengths, cache_values)
    piece = lax.dynamic_index_in_dim(exchange(mine, PLANE), span_owner[0] // 2, 0, False)
    piece, values = lax.optimization_barrier((piece, values))

    own_away = exchange(jnp.broadcast_to(piece[None], (PIECES, PIECE, HEAD)), TEAMS)
    other_away = lax.ppermute(own_away, AXIS, SWAP)
    own_here = lax.ppermute(own_away, AXIS, PAIR)

    cache_keys = pltpu.with_memory_space_constraint(cache_keys, pltpu.HBM)
    part, keys = attention(own_away, cache_keys, values, first=True)
    part, other_away, own_here, keys = lax.optimization_barrier((part, other_away, own_here, keys))
    here_1 = lax.ppermute(part, AXIS, PAIR)
    other_here = lax.ppermute(own_here, AXIS, SWAP)
    part = attention(other_away, keys, values)
    part, other_here = lax.optimization_barrier((part, other_here))
    here_2 = lax.ppermute(part, AXIS, CROSS)
    part = attention(other_here, keys, values)
    part, own_here = lax.optimization_barrier((part, own_here))
    here_3 = lax.ppermute(part, AXIS, SWAP)
    part = attention(own_here, keys, values)

    received = exchange(merge(part, here_3, merge(here_1, here_2)), TEAMS)
    result = exchange(finish(received), PLANE)
    out = place(span_owner, result, lax.ppermute(result, AXIS, SWAP))
    return out[None]


def solution(mesh):
    return jax.shard_map(
        per_device,
        mesh=mesh,
        in_specs=(P("seq", None, "head"), P("seq", "head"), P("seq", "head"), P(), P()),
        out_specs=P("seq", None, "head"),
        check_vma=False,
    )
```

time: 92.6 us -> 110 us (1.19)
  starting transfers between devices: 13.8 us -> 37.1 us
  blocking collectives: 38 us -> 32.5 us
  local copies, waits for them, and re-layouts: 7.83 us -> 3.31 us
  waiting for transfers between devices: 2.52 us -> 5.58 us
  Pallas kernels: 29.2 us -> 30.4 us
    ppermute x4 -> x8, starting transfers between devices: 8.77 us -> 32 us  [the longest x1 13 us: per_device(): out = place(span_owner, result, lax.ppermute(result, AXIS, SWAP))]
    all_to_all x3, blocking collectives: 38 us -> 32.5 us  [exchange(): lax.all_to_all(pieces, AXIS, 0, 0, axis_index_groups=groups, tiled=True)]
    unnamed x12 -> x6, local copies, waits for them, and re-layouts: 7.78 us -> 3.28 us
    all_to_all x1, waiting for transfers between devices: 0.84 us -> 3.89 us  [exchange(): lax.all_to_all(pieces, AXIS, 0, 0, axis_index_groups=groups, tiled=True)]
    pallas_call x6 -> x8, Pallas kernels: 28.3 us -> 29.6 us  [the longest x4 26.7 us: attention(): pl.pallas_call(first_attention_kernel if first else attention_kernel, out...]
  transfers between devices with their start and end apart: 5 -> 9, of which waited for: 3 -> 3; matrix products, arithmetic and copies ran while one was open for 0% -> 0% of each run, Pallas kernels for 10% -> 26%
where the time goes in v1:
time: 110 us
  starting transfers between devices  37.1 us (34%)
  blocking collectives  32.5 us (30%)
  Pallas kernels  30.4 us (28%)
  waiting for transfers between devices  5.58 us (5%)
  local copies, waits for them, and re-layouts  3.31 us (3%)
    all_to_all x3, blocking collectives, exchange(): lax.all_to_all(pieces, AXIS, 0, 0, axis_index_groups=groups, tiled=True)  32.5 us
    pallas_call x4, Pallas kernels, attention(): pl.pallas_call(first_attention_kernel if first else attention_kernel, out...  26.7 us
    ppermute x1, starting transfers between devices, per_device(): out = place(span_owner, result, lax.ppermute(result, AXIS, SWAP))  13 us
    ppermute x1, starting transfers between devices, per_device(): here_1 = lax.ppermute(part, AXIS, PAIR)  11 us
    all_to_all x1, starting transfers between devices, exchange(): lax.all_to_all(pieces, AXIS, 0, 0, axis_index_groups=groups, tiled=True)  5.02 us
    all_to_all x1, waiting for transfers between devices, exchange(): lax.all_to_all(pieces, AXIS, 0, 0, axis_index_groups=groups, tiled=True)  3.89 us
    ppermute x1, starting transfers between devices, per_device(): mine = choose(span_owner, keep, lax.ppermute(send, AXIS, SWAP))  3.33 us
    unnamed x6, local copies, waits for them, and re-layouts  3.28 us
  transfers between devices with their start and end apart: 9, of which 3 were waited for; matrix products, arithmetic and copies ran while one was open for 0% of the time, Pallas kernels for 26%

profile of v1, /device:TPU:1, one launch (start us, length us, event | category | flops | bytes accessed | tf_op | source)
XLA Modules:
  0.0 109.7 jit_solution(10108170274131166518)
XLA Ops:
  0.0 1.0 copy-done.1
  1.1 3.3 %collective-permute-start = (bf16[16,64,128]{2,1,0:T(8,128)(2,1)S(1)}, bf16[16,64,128]{2,1,0:T(8,128)(2,1)S(1)}, u32[]{:S(2)}, u32[]{:S(2)}) collective-permute-start(bf16[16,64,128]{2,1,0:T(8,128)(2,1)S(1)} %get-tuple-element.22), channel_id=1, source_target_pairs={{0,8},{8,0},{16,24},{24,16},{32,40},{40,32},{48,56},{56,48},{64,72... | collective-permute-start | bytes 786440 | tf_op jit(solution)/shard_map/ppermute | solution.py:320
  5.1 0.5 collective-permute-done.b_ref
  5.6 0.7 choose.1
  6.4 5.0 %all-to-all-start = ((bf16[16,64,128]{2,1,0:T(8,128)(2,1)}), bf16[16,64,128]{2,1,0:T(8,128)(2,1)S(1)}, u32[]{:S(2)}, u32[]{:S(2)}) async-start(bf16[16,64,128]{2,1,0:T(8,128)(2,1)} %choose.1), calls=%async_computation | async-start | bytes 524288 | tf_op jit(solution)/shard_map/all_to_all | solution.py:60
  11.4 1.6 %copy-done = bf16[8192,128]{1,0:T(8,128)(2,1)S(1)} copy-done((bf16[8192,128]{1,0:T(8,128)(2,1)S(1)}, bf16[8192,128]{1,0:T(8,128)(2,1)}, u32[]{:S(2)}) %copy-start) | copy-done | bytes 2097176
  13.0 0.7 copy-done.2
  13.7 1.9 %turn_values.1.v_ref = bf16[144,8192]{1,0:T(8,128)(2,1)S(1)} custom-call(s32[32]{0:T(128)S(1)} %copy-done.2, bf16[8192,128]{1,0:T(8,128)(2,1)S(1)} %copy-done), custom_call_target="tpu_custom_call" | custom-call | flops 536870912 | bytes 5242880 | tf_op jit(solution)/shard_map/turn_values/pallas_call | solution.py:77
  15.6 3.9 %all-to-all-done = bf16[16,64,128]{2,1,0:T(8,128)(2,1)S(1)} async-done(((bf16[16,64,128]{2,1,0:T(8,128)(2,1)}), bf16[16,64,128]{2,1,0:T(8,128)(2,1)S(1)}, u32[]{:S(2)}, u32[]{:S(2)}) %all-to-all-start) | async-done | bytes 262176 | tf_op jit(solution)/shard_map/all_to_all | solution.py:60
  19.5 9.6 %all_to_all.20 = bf16[8,64,128]{2,1,0:T(8,128)(2,1)S(1)} all-to-all(bf16[8,64,128]{2,1,0:T(8,128)(2,1)S(1)} %broadcast_in_dim.4), channel_id=1, replica_groups={{0,32,64,96,128,160,192,224},{16,48,80,112,144,176,208,240},{8,40,72,10..., dimensions={0} | all-to-all | bytes 262144 | tf_op jit(solution)/shard_map/all_to_all | solution.py:60
  29.1 2.9 %collective-permute-start.1 = (bf16[8,64,128]{2,1,0:T(8,128)(2,1)S(1)}, bf16[8,64,128]{2,1,0:T(8,128)(2,1)S(1)}, u32[]{:S(2)}, u32[]{:S(2)}) collective-permute-start(bf16[8,64,128]{2,1,0:T(8,128)(2,1)S(1)} %all_to_all.20), channel_id=1, source_target_pairs={{0,8},{8,0},{16,24},{24,16},{32,40},{40,32},{48,56},{56,48},{64,72... | collective-permute-start | bytes 393224 | tf_op jit(solution)/shard_map/ppermute | solution.py:327
  32.0 0.3 collective-permute-start.2
  32.3 5.0 %attention.4 = (f32[8,72,128]{2,1,0:T(8,128)S(1)}, bf16[8192,128]{1,0:T(8,128)(2,1)S(1)}) custom-call(bf16[512,128]{1,0:T(8,128)(2,1)S(1)} %bitcast.13, bf16[8192,128]{1,0:T(8,128)(2,1)} %k_ref.1, bf16[144,8192]{1,0:T(8,128)(2,1)S(1)} %turn_values.1.v_ref), custom_call_target="tpu_custom_call" | custom-call | flops 268435456 | bytes 1048576 | tf_op jit(solution)/shard_map/attention/pallas_call | solution.py:165
  37.4 0.5 collective-permute-start.3
  37.9 11.0 %collective-permute-start.5 = (f32[8,72,128]{2,1,0:T(8,128)S(1)}, f32[8,72,128]{2,1,0:T(8,128)S(1)}, u32[]{:S(2)}, u32[]{:S(2)}) collective-permute-start(f32[8,72,128]{2,1,0:T(8,128)S(1)} %get-tuple-element.35), channel_id=1, source_target_pairs={{0,16},{8,56},{16,0},{24,40},{32,48},{40,24},{48,32},{56,8},{64,80... | collective-permute-start | bytes 884744 | tf_op jit(solution)/shard_map/ppermute | solution.py:333
  48.9 3.7 %attention.5 = f32[8,72,128]{2,1,0:T(8,128)S(1)} custom-call(bf16[512,128]{1,0:T(8,128)(2,1)S(1)} %bitcast.16, bf16[8192,128]{1,0:T(8,128)(2,1)S(1)} %get-tuple-element.30.k_ref, bf16[144,8192]{1,0:T(8,128)(2,1)S(1)} %turn_values.1.v_ref), custom_call_target="tpu_custom_call" | custom-call | flops 268435456 | bytes 1048576 | tf_op jit(solution)/shard_map/attention/pallas_call | solution.py:165
  52.5 1.0 collective-permute-start.6
  53.5 14.3 %attention.6 = f32[8,72,128]{2,1,0:T(8,128)S(1)} custom-call(bf16[512,128]{1,0:T(8,128)(2,1)S(1)} %bitcast.17, bf16[8192,128]{1,0:T(8,128)(2,1)S(1)} %get-tuple-element.30.k_ref, bf16[144,8192]{1,0:T(8,128)(2,1)S(1)} %turn_values.1.v_ref), custom_call_target="tpu_custom_call" | custom-call | flops 268435456 | bytes 1048576 | tf_op jit(solution)/shard_map/attention/pallas_call | solution.py:165
  67.9 3.7 %attention.7.refs_0_ = f32[8,72,128]{2,1,0:T(8,128)S(1)} custom-call(bf16[512,128]{1,0:T(8,128)(2,1)S(1)} %bitcast.15, bf16[8192,128]{1,0:T(8,128)(2,1)S(1)} %get-tuple-element.30.k_ref, bf16[144,8192]{1,0:T(8,128)(2,1)S(1)} %turn_values.1.v_ref), custom_call_target="tpu_custom_call" | custom-call | flops 268435456 | bytes 1048576 | tf_op jit(solution)/shard_map/attention/pallas_call | solution.py:165
  71.8 11.9 %all_to_all.21.r_ref = f32[8,72,128]{2,1,0:T(8,128)S(1)} all-to-all(f32[8,72,128]{2,1,0:T(8,128)S(1)} %merge.3), channel_id=1, replica_groups={{0,32,64,96,128,160,192,224},{16,48,80,112,144,176,208,240},{8,40,72,10..., dimensions={0} | all-to-all | bytes 589824 | tf_op jit(solution)/shard_map/all_to_all | solution.py:60
  83.7 11.0 %all_to_all.22.a_ref = bf16[16,64,128]{2,1,0:T(8,128)(2,1)S(1)} all-to-all(bf16[16,64,128]{2,1,0:T(8,128)(2,1)S(1)} %finish.1), channel_id=1, replica_groups={{0,16,32,48,64,80,96,112,128,144,160,176,192,208,224,240},{8,24,40,56,7..., dimensions={0} | all-to-all | bytes 524288 | tf_op jit(solution)/shard_map/all_to_all | solution.py:60
  94.7 13.0 %collective-permute-start.7 = (bf16[16,64,128]{2,1,0:T(8,128)(2,1)S(1)}, bf16[16,64,128]{2,1,0:T(8,128)(2,1)S(1)}, u32[]{:S(2)}, u32[]{:S(2)}) collective-permute-start(bf16[16,64,128]{2,1,0:T(8,128)(2,1)S(1)} %all_to_all.22.a_ref), channel_id=1, source_target_pairs={{0,8},{8,0},{16,24},{24,16},{32,40},{40,32},{48,56},{56,48},{64,72... | collective-permute-start | bytes 786440 | tf_op jit(solution)/shard_map/ppermute | solution.py:345
  107.7 1.2 %collective-permute-done.7.b_ref = bf16[16,64,128]{2,1,0:T(8,128)(2,1)S(1)} collective-permute-done((bf16[16,64,128]{2,1,0:T(8,128)(2,1)S(1)}, bf16[16,64,128]{2,1,0:T(8,128)(2,1)S(1)}, u32[]{:S(2)}, u32[]{:S(2)}) %collective-permute-start.7) | collective-permute-done | bytes 262176 | tf_op jit(solution)/shard_map/ppermute | solution.py:345
  108.8 0.8 place.1
  (16 shorter events, 0.4 us)
Async XLA Ops:
  0.0 1.0 copy-start.1
  1.1 4.5 %collective-permute-start = (bf16[16,64,128]{2,1,0:T(8,128)(2,1)S(1)}, bf16[16,64,128]{2,1,0:T(8,128)(2,1)S(1)}, u32[]{:S(2)}, u32[]{:S(2)}) collective-permute-start(bf16[16,64,128]{2,1,0:T(8,128)(2,1)S(1)} %get-tuple-element.22), channel_id=1, source_target_pairs={{0,8},{8,0},{16,24},{24,16},{32,40},{40,32},{48,56},{56,48},{64,72... | collective-permute-start | bytes 786440 | tf_op jit(solution)/shard_map/ppermute | solution.py:320
  6.4 13.1 %all-to-all-start = ((bf16[16,64,128]{2,1,0:T(8,128)(2,1)}), bf16[16,64,128]{2,1,0:T(8,128)(2,1)S(1)}, u32[]{:S(2)}, u32[]{:S(2)}) async-start(bf16[16,64,128]{2,1,0:T(8,128)(2,1)} %choose.1), calls=%async_computation | async-start | bytes 524288 | tf_op jit(solution)/shard_map/all_to_all | solution.py:60
  11.4 1.6 %copy-start = (bf16[8192,128]{1,0:T(8,128)(2,1)S(1)}, bf16[8192,128]{1,0:T(8,128)(2,1)}, u32[]{:S(2)}) copy-start(bf16[8192,128]{1,0:T(8,128)(2,1)} %v_ref.1) | copy-start | bytes 6291460
  13.0 0.7 copy-start.2
  29.1 8.3 %collective-permute-start.1 = (bf16[8,64,128]{2,1,0:T(8,128)(2,1)S(1)}, bf16[8,64,128]{2,1,0:T(8,128)(2,1)S(1)}, u32[]{:S(2)}, u32[]{:S(2)}) collective-permute-start(bf16[8,64,128]{2,1,0:T(8,128)(2,1)S(1)} %all_to_all.20), channel_id=1, source_target_pairs={{0,8},{8,0},{16,24},{24,16},{32,40},{40,32},{48,56},{56,48},{64,72... | collective-permute-start | bytes 393224 | tf_op jit(solution)/shard_map/ppermute | solution.py:327
  32.0 5.4 %collective-permute-start.2 = (bf16[8,64,128]{2,1,0:T(8,128)(2,1)S(1)}, bf16[8,64,128]{2,1,0:T(8,128)(2,1)S(1)}, u32[]{:S(2)}, u32[]{:S(2)}) collective-permute-start(bf16[8,64,128]{2,1,0:T(8,128)(2,1)S(1)} %all_to_all.20), channel_id=1, source_target_pairs={{0,16},{8,56},{16,0},{24,40},{32,48},{40,24},{48,32},{56,8},{64,80... | collective-permute-start | bytes 393224 | tf_op jit(solution)/shard_map/ppermute | solution.py:328
  37.4 15.1 %collective-permute-start.3 = (bf16[8,64,128]{2,1,0:T(8,128)(2,1)S(1)}, bf16[8,64,128]{2,1,0:T(8,128)(2,1)S(1)}, u32[]{:S(2)}, u32[]{:S(2)}) collective-permute-start(bf16[8,64,128]{2,1,0:T(8,128)(2,1)S(1)} %collective-permute-done.2), channel_id=1, source_target_pairs={{0,8},{8,0},{16,24},{24,16},{32,40},{40,32},{48,56},{56,48},{64,72... | collective-permute-start | bytes 393224 | tf_op jit(solution)/shard_map/ppermute | solution.py:334
  37.9 33.7 %collective-permute-start.5 = (f32[8,72,128]{2,1,0:T(8,128)S(1)}, f32[8,72,128]{2,1,0:T(8,128)S(1)}, u32[]{:S(2)}, u32[]{:S(2)}) collective-permute-start(f32[8,72,128]{2,1,0:T(8,128)S(1)} %get-tuple-element.35), channel_id=1, source_target_pairs={{0,16},{8,56},{16,0},{24,40},{32,48},{40,24},{48,32},{56,8},{64,80... | collective-permute-start | bytes 884744 | tf_op jit(solution)/shard_map/ppermute | solution.py:333
  52.5 19.1 %collective-permute-start.6 = (f32[8,72,128]{2,1,0:T(8,128)S(1)}, f32[8,72,128]{2,1,0:T(8,128)S(1)}, u32[]{:S(2)}, u32[]{:S(2)}) collective-permute-start(f32[8,72,128]{2,1,0:T(8,128)S(1)} %attention.5), channel_id=1, source_target_pairs={{8,16},{0,56},{24,0},{16,40},{40,48},{32,24},{56,32},{48,8},{72,80... | collective-permute-start | bytes 884744 | tf_op jit(solution)/shard_map/ppermute | solution.py:337
  67.8 3.9 %collective-permute-start.4 = (f32[8,72,128]{2,1,0:T(8,128)S(1)}, f32[8,72,128]{2,1,0:T(8,128)S(1)}, u32[]{:S(2)}, u32[]{:S(2)}) collective-permute-start(f32[8,72,128]{2,1,0:T(8,128)S(1)} %attention.6), channel_id=1, source_target_pairs={{0,8},{8,0},{16,24},{24,16},{32,40},{40,32},{48,56},{56,48},{64,72... | collective-permute-start | bytes 884744 | tf_op jit(solution)/shard_map/ppermute | solution.py:340
  94.7 14.1 %collective-permute-start.7 = (bf16[16,64,128]{2,1,0:T(8,128)(2,1)S(1)}, bf16[16,64,128]{2,1,0:T(8,128)(2,1)S(1)}, u32[]{:S(2)}, u32[]{:S(2)}) collective-permute-start(bf16[16,64,128]{2,1,0:T(8,128)(2,1)S(1)} %all_to_all.22.a_ref), channel_id=1, source_target_pairs={{0,8},{8,0},{16,24},{24,16},{32,40},{40,32},{48,56},{56,48},{64,72... | collective-permute-start | bytes 786440 | tf_op jit(solution)/shard_map/ppermute | solution.py:345

commit v2 on v1

--- a/solution.py
+++ b/solution.py
@@ -19,7 +19,7 @@
 BLOCK = 512
 PIECES = 2 * BLOCK // HEAD
 STEP = 512
-CHUNKS = 4
+CHUNK = 2048
 BF16 = jnp.bfloat16
 F32 = jnp.float32
 LOG2_SCALE = math.log2(math.e) / math.sqrt(HEAD)
@@ -60,8 +60,13 @@
     return lax.all_to_all(pieces, AXIS, 0, 0, axis_index_groups=groups, tiled=True)
 
 
-def values_kernel(len_ref, v_ref, o_ref):
+def values_kernel(len_ref, k_ref, v_ref, head_ref, o_ref):
     size = v_ref.shape[0]
+
+    @pl.when(pl.program_id(0) == 0)
+    def _():
+        head_ref[...] = k_ref[...]
+
     lanes = lax.broadcasted_iota(jnp.int32, (HEAD, HEAD), 1)
     eye = (lanes == lax.broadcasted_iota(jnp.int32, (HEAD, HEAD), 0)).astype(BF16)
     turned = lax.dot_general(eye, v_ref[...], NT, preferred_element_type=F32)
@@ -71,24 +76,27 @@
     o_ref[HEAD:, :] = jnp.broadcast_to(jnp.where(valid, 1.0, 0.0), (16, size)).astype(BF16)
 
 
-def turned_values(lengths, values):
-    keys = values.shape[0]
-    size = 2048
+def turned_values(lengths, keys, values):
+    count = values.shape[0]
+    head = pl.BlockSpec((CHUNK, HEAD), lambda i, n: (0, 0))
     return pl.pallas_call(
         values_kernel,
-        out_shape=jax.ShapeDtypeStruct((VROWS, keys), BF16),
+        out_shape=(
+            jax.ShapeDtypeStruct((CHUNK, HEAD), BF16),
+            jax.ShapeDtypeStruct((VROWS, count), BF16),
+        ),
         grid_spec=pltpu.PrefetchScalarGridSpec(
             num_scalar_prefetch=1,
-            grid=(keys // size,),
-            in_specs=[pl.BlockSpec((size, HEAD), lambda i, n: (i, 0))],
-            out_specs=pl.BlockSpec((VROWS, size), lambda i, n: (0, i)),
+            grid=(count // CHUNK,),
+            in_specs=[head, pl.BlockSpec((CHUNK, HEAD), lambda i, n: (i, 0))],
+            out_specs=(head, pl.BlockSpec((VROWS, CHUNK), lambda i, n: (0, i))),
         ),
         compiler_params=vmem(16),
         cost_estimate=pl.CostEstimate(
-            flops=4 * keys * HEAD * HEAD, bytes_accessed=5 * keys * HEAD, transcendentals=0
+            flops=4 * count * HEAD * HEAD, bytes_accessed=5 * count * HEAD, transcendentals=0
         ),
         name="turn_values",
-    )(lengths, values)
+    )(lengths, pltpu.with_memory_space_constraint(keys, pltpu.HBM), values)
 
 
 def write_block(o_ref, out, sums, top):
@@ -140,34 +148,53 @@
     settle(weigh(q, k_ref[...], v_ref[...]), q, k_ref, v_ref, o_ref, acc_ref)
 
 
-def first_attention_kernel(q_ref, k_ref, v_ref, o_ref, kept_ref, acc_ref, sems):
-    size = k_ref.shape[0] // CHUNKS
-    spans = [slice(i * size, (i + 1) * size) for i in range(CHUNKS)]
+def first_attention_kernel(q_ref, head_ref, k_ref, v_ref, o_ref, kept_ref, acc_ref, sems):
+    spans = [slice(start, start + CHUNK) for start in range(0, k_ref.shape[0], CHUNK)]
     copies = [
-        pltpu.make_async_copy(k_ref.at[span], kept_ref.at[span], sems.at[i])
+        pltpu.make_async_copy(k_ref.at[span] if i else head_ref, kept_ref.at[span], sems.at[i])
         for i, span in enumerate(spans)
     ]
-    for copy in copies:
+    for copy in copies[1:] + copies[:1]:
         copy.start()
     q = q_ref[...]
-    total = None
-    for copy, span in zip(copies, spans):
+    total = weigh(q, head_ref[...], v_ref[:, spans[0]])
+    for copy, span in zip(copies[1:], spans[1:]):
         copy.wait()
-        part = weigh(q, kept_ref[span, :], v_ref[:, span])
-        total = part if total is None else total + part
+        total += weigh(q, kept_ref[span, :], v_ref[:, span])
+    copies[0].wait()
     settle(total, q, kept_ref, v_ref, o_ref, acc_ref)
 
 
-def attention(rows, keys, values, first=False):
+def first_attention(rows, head, keys, values):
     vmem_spec = pl.BlockSpec(memory_space=pltpu.VMEM)
-    out = jax.ShapeDtypeStruct((PIECES, ROWS, HEAD), F32)
-    scratch = [pltpu.VMEM((VROWS, BLOCK), F32)]
-    return pl.pallas_call(
-        first_attention_kernel if first else attention_kernel,
-        out_shape=(out, jax.ShapeDtypeStruct(keys.shape, BF16)) if first else out,
-        in_specs=[vmem_spec, pl.BlockSpec(memory_space=pltpu.HBM) if first else vmem_spec, vmem_spec],
-        out_specs=(vmem_spec, vmem_spec) if first else vmem_spec,
-        scratch_shapes=scratch + ([pltpu.SemaphoreType.DMA((CHUNKS,))] if first else []),
+    return pl.pallas_call(
+        first_attention_kernel,
+        out_shape=(
+            jax.ShapeDtypeStruct((PIECES, ROWS, HEAD), F32),
+            jax.ShapeDtypeStruct(keys.shape, BF16),
+        ),
+        in_specs=[vmem_spec, vmem_spec, pl.BlockSpec(memory_space=pltpu.HBM), vmem_spec],
+        out_specs=(vmem_spec, vmem_spec),
+        scratch_shapes=[
+            pltpu.VMEM((VROWS, BLOCK), F32),
+            pltpu.SemaphoreType.DMA((keys.shape[0] // CHUNK,)),
+        ],
+        compiler_params=vmem(44),
+        cost_estimate=pl.CostEstimate(
+            flops=BLOCK * keys.size // 2, bytes_accessed=keys.size, transcendentals=0
+        ),
+        name="first_attention",
+    )(rows.reshape(BLOCK, HEAD), head, pltpu.with_memory_space_constraint(keys, pltpu.HBM), values)
+
+
+def attention(rows, keys, values):
+    vmem_spec = pl.BlockSpec(memory_space=pltpu.VMEM)
+    return pl.pallas_call(
+        attention_kernel,
+        out_shape=jax.ShapeDtypeStruct((PIECES, ROWS, HEAD), F32),
+        in_specs=[vmem_spec] * 3,
+        out_specs=vmem_spec,
+        scratch_shapes=[pltpu.VMEM((VROWS, BLOCK), F32)],
         compiler_params=vmem(44),
         cost_estimate=pl.CostEstimate(
             flops=BLOCK * keys.size // 2, bytes_accessed=keys.size, transcendentals=0
@@ -319,28 +346,29 @@
     keep, send = split(queries[0])
     mine = choose(span_owner, keep, lax.ppermute(send, AXIS, SWAP))
     lengths, mine = lax.optimization_barrier((lengths, mine))
-    values = turned_values(lengths, cache_values)
+    first_keys, values = turned_values(lengths, cache_keys, cache_values)
     piece = lax.dynamic_index_in_dim(exchange(mine, PLANE), span_owner[0] // 2, 0, False)
-    piece, values = lax.optimization_barrier((piece, values))
+    piece, first_keys, values = lax.optimization_barrier((piece, first_keys, values))
 
     own_away = exchange(jnp.broadcast_to(piece[None], (PIECES, PIECE, HEAD)), TEAMS)
     other_away = lax.ppermute(own_away, AXIS, SWAP)
     own_here = lax.ppermute(own_away, AXIS, PAIR)
 
-    cache_keys = pltpu.with_memory_space_constraint(cache_keys, pltpu.HBM)
-    part, keys = attention(own_away, cache_keys, values, first=True)
-    part, other_away, own_here, keys = lax.optimization_barrier((part, other_away, own_here, keys))
-    here_1 = lax.ppermute(part, AXIS, PAIR)
+    part, keys = first_attention(own_away, first_keys, cache_keys, values)
+    attend = functools.partial(attention, keys=keys, values=values)
+    part, other_away, own_here = lax.optimization_barrier((part, other_away, own_here))
+    peer_away = lax.ppermute(part, AXIS, SWAP)
     other_here = lax.ppermute(own_here, AXIS, SWAP)
-    part = attention(other_away, keys, values)
-    part, other_here = lax.optimization_barrier((part, other_here))
-    here_2 = lax.ppermute(part, AXIS, CROSS)
-    part = attention(other_here, keys, values)
+    part = attend(other_away)
+    away = merge(part, peer_away)
+    away, other_here = lax.optimization_barrier((away, other_here))
+    here = lax.ppermute(away, AXIS, CROSS)
+    part = attend(other_here)
+    peer_here = lax.ppermute(part, AXIS, SWAP)
     part, own_here = lax.optimization_barrier((part, own_here))
-    here_3 = lax.ppermute(part, AXIS, SWAP)
-    part = attention(own_here, keys, values)
-
-    received = exchange(merge(part, here_3, merge(here_1, here_2)), TEAMS)
+    part = attend(own_here)
+
+    received = exchange(merge(part, peer_here, merge(here)), TEAMS)
     result = exchange(finish(received), PLANE)
     out = place(span_owner, result, lax.ppermute(result, AXIS, SWAP))
     return out[None]

time: 110 us -> 110 us (level)
  transfers between devices with their start and end apart: 9 -> 9, of which waited for: 3 -> 4; matrix products, arithmetic and copies ran while one was open for 0% -> 0% of each run, Pallas kernels for 26% -> 27%
where the time goes in v2:
time: 110 us
  starting transfers between devices  36.2 us (33%)
  blocking collectives  33.2 us (30%)
  Pallas kernels  31.1 us (28%)
  waiting for transfers between devices  4.94 us (4%)
  local copies, waits for them, and re-layouts  3.31 us (3%)
    all_to_all x3, blocking collectives, exchange(): lax.all_to_all(pieces, AXIS, 0, 0, axis_index_groups=groups, tiled=True)  33.2 us
    pallas_call x3, Pallas kernels, attention(): pl.pallas_call(attention_kernel, out_shape=jax.ShapeDtypeStruct((PIECES,...  21.8 us
    ppermute x1, starting transfers between devices, per_device(): out = place(span_owner, result, lax.ppermute(result, AXIS, SWAP))  12.9 us
    ppermute x1, starting transfers between devices, per_device(): here = lax.ppermute(away, AXIS, CROSS)  11.8 us
    all_to_all x1, starting transfers between devices, exchange(): lax.all_to_all(pieces, AXIS, 0, 0, axis_index_groups=groups, tiled=True)  5.02 us
    pallas_call x1, Pallas kernels, first_attention(): pl.pallas_call(first_attention_kernel, out_shape=(jax.ShapeDtypeStruct((P...  4.39 us
    ppermute x1, starting transfers between devices, per_device(): mine = choose(span_owner, keep, lax.ppermute(send, AXIS, SWAP))  3.33 us
    unnamed x6, local copies, waits for them, and re-layouts  3.28 us
  transfers between devices with their start and end apart: 9, of which 4 were waited for; matrix products, arithmetic and copies ran while one was open for 0% of the time, Pallas kernels for 27%

profile of v2, /device:TPU:1, one launch (start us, length us, event | category | flops | bytes accessed | tf_op | source)
XLA Modules:
  0.0 109.6 jit_solution(15147412584428951419)
XLA Ops:
  0.0 1.0 copy-done.1
  1.1 3.3 %collective-permute-start = (bf16[16,64,128]{2,1,0:T(8,128)(2,1)S(1)}, bf16[16,64,128]{2,1,0:T(8,128)(2,1)S(1)}, u32[]{:S(2)}, u32[]{:S(2)}) collective-permute-start(bf16[16,64,128]{2,1,0:T(8,128)(2,1)S(1)} %get-tuple-element.23), channel_id=1, source_target_pairs={{0,8},{8,0},{16,24},{24,16},{32,40},{40,32},{48,56},{56,48},{64,72... | collective-permute-start | bytes 786440 | tf_op jit(solution)/shard_map/ppermute | solution.py:347
  5.1 0.5 collective-permute-done.b_ref
  5.6 0.7 choose.1
  6.4 5.0 %all-to-all-start = ((bf16[16,64,128]{2,1,0:T(8,128)(2,1)}), bf16[16,64,128]{2,1,0:T(8,128)(2,1)S(1)}, u32[]{:S(2)}, u32[]{:S(2)}) async-start(bf16[16,64,128]{2,1,0:T(8,128)(2,1)} %choose.1), calls=%async_computation | async-start | bytes 524288 | tf_op jit(solution)/shard_map/all_to_all | solution.py:60
  11.4 1.6 %copy-done = bf16[8192,128]{1,0:T(8,128)(2,1)S(1)} copy-done((bf16[8192,128]{1,0:T(8,128)(2,1)S(1)}, bf16[8192,128]{1,0:T(8,128)(2,1)}, u32[]{:S(2)}) %copy-start) | copy-done | bytes 2097176
  13.0 0.7 copy-done.2
  13.7 3.0 %turn_values.1 = (bf16[2048,128]{1,0:T(8,128)(2,1)S(1)}, bf16[144,8192]{1,0:T(8,128)(2,1)S(1)}) custom-call(s32[32]{0:T(128)S(1)} %copy-done.2, bf16[8192,128]{1,0:T(8,128)(2,1)} %k_ref.3, bf16[8192,128]{1,0:T(8,128)(2,1)S(1)} %copy-done), custom_call_target="tpu_custom_call" | custom-call | flops 536870912 | bytes 5242880 | tf_op jit(solution)/shard_map/turn_values/pallas_call | solution.py:82
  16.7 2.8 %all-to-all-done = bf16[16,64,128]{2,1,0:T(8,128)(2,1)S(1)} async-done(((bf16[16,64,128]{2,1,0:T(8,128)(2,1)}), bf16[16,64,128]{2,1,0:T(8,128)(2,1)S(1)}, u32[]{:S(2)}, u32[]{:S(2)}) %all-to-all-start) | async-done | bytes 262176 | tf_op jit(solution)/shard_map/all_to_all | solution.py:60
  19.5 10.6 %all_to_all.20 = bf16[8,64,128]{2,1,0:T(8,128)(2,1)S(1)} all-to-all(bf16[8,64,128]{2,1,0:T(8,128)(2,1)S(1)} %broadcast_in_dim.4), channel_id=1, replica_groups={{0,32,64,96,128,160,192,224},{16,48,80,112,144,176,208,240},{8,40,72,10..., dimensions={0} | all-to-all | bytes 262144 | tf_op jit(solution)/shard_map/all_to_all | solution.py:60
  30.1 2.4 %collective-permute-start.1 = (bf16[8,64,128]{2,1,0:T(8,128)(2,1)S(1)}, bf16[8,64,128]{2,1,0:T(8,128)(2,1)S(1)}, u32[]{:S(2)}, u32[]{:S(2)}) collective-permute-start(bf16[8,64,128]{2,1,0:T(8,128)(2,1)S(1)} %all_to_all.20), channel_id=1, source_target_pairs={{0,8},{8,0},{16,24},{24,16},{32,40},{40,32},{48,56},{56,48},{64,72... | collective-permute-start | bytes 393224 | tf_op jit(solution)/shard_map/ppermute | solution.py:354
  32.5 0.2 collective-permute-start.2
  32.6 4.4 %first_attention.1 = (f32[8,72,128]{2,1,0:T(8,128)S(1)}, bf16[8192,128]{1,0:T(8,128)(2,1)S(1)}) custom-call(bf16[512,128]{1,0:T(8,128)(2,1)S(1)} %bitcast.13, bf16[2048,128]{1,0:T(8,128)(2,1)S(1)} %get-tuple-element.29.head_ref, bf16[8192,128]{1,0:T(8,128)(2,1)} %k_ref.3, bf16[144,8192]{1,0:T(8,128)(2,1)S(1)} %get-tuple-element.30.v_ref), custom_call_target="tpu_custom_call" | custom-call | flops 268435456 | bytes 1048576 | tf_op jit(solution)/shard_map/first_attention/pallas_call | solution.py:170
  37.1 0.4 collective-permute-done.2
  37.5 0.5 collective-permute-start.4
  38.0 3.9 %attention.3.refs_0_ = f32[8,72,128]{2,1,0:T(8,128)S(1)} custom-call(bf16[512,128]{1,0:T(8,128)(2,1)S(1)} %bitcast.16, bf16[8192,128]{1,0:T(8,128)(2,1)S(1)} %get-tuple-element.33.k_ref, bf16[144,8192]{1,0:T(8,128)(2,1)S(1)} %get-tuple-element.30.v_ref), custom_call_target="tpu_custom_call" | custom-call | flops 268435456 | bytes 1048576 | tf_op jit(solution)/shard_map/attention/pallas_call | solution.py:192
  42.0 11.8 %collective-permute-start.6 = (f32[8,72,128]{2,1,0:T(8,128)S(1)}, f32[8,72,128]{2,1,0:T(8,128)S(1)}, u32[]{:S(2)}, u32[]{:S(2)}) collective-permute-start(f32[8,72,128]{2,1,0:T(8,128)S(1)} %merge.3), channel_id=1, source_target_pairs={{8,16},{0,56},{24,0},{16,40},{40,48},{32,24},{56,32},{48,8},{72,80... | collective-permute-start | bytes 884744 | tf_op jit(solution)/shard_map/ppermute | solution.py:365
  53.8 14.3 %attention.4 = f32[8,72,128]{2,1,0:T(8,128)S(1)} custom-call(bf16[512,128]{1,0:T(8,128)(2,1)S(1)} %bitcast.17, bf16[8192,128]{1,0:T(8,128)(2,1)S(1)} %get-tuple-element.33.k_ref, bf16[144,8192]{1,0:T(8,128)(2,1)S(1)} %get-tuple-element.30.v_ref), custom_call_target="tpu_custom_call" | custom-call | flops 268435456 | bytes 1048576 | tf_op jit(solution)/shard_map/attention/pallas_call | solution.py:192
  68.2 3.7 %attention.5.refs_0_ = f32[8,72,128]{2,1,0:T(8,128)S(1)} custom-call(bf16[512,128]{1,0:T(8,128)(2,1)S(1)} %bitcast.15, bf16[8192,128]{1,0:T(8,128)(2,1)S(1)} %get-tuple-element.33.k_ref, bf16[144,8192]{1,0:T(8,128)(2,1)S(1)} %get-tuple-element.30.v_ref), custom_call_target="tpu_custom_call" | custom-call | flops 268435456 | bytes 1048576 | tf_op jit(solution)/shard_map/attention/pallas_call | solution.py:192
  72.0 11.6 %all_to_all.21.r_ref = f32[8,72,128]{2,1,0:T(8,128)S(1)} all-to-all(f32[8,72,128]{2,1,0:T(8,128)S(1)} %merge.5), channel_id=1, replica_groups={{0,32,64,96,128,160,192,224},{16,48,80,112,144,176,208,240},{8,40,72,10..., dimensions={0} | all-to-all | bytes 589824 | tf_op jit(solution)/shard_map/all_to_all | solution.py:60
  83.6 11.1 %all_to_all.22.a_ref = bf16[16,64,128]{2,1,0:T(8,128)(2,1)S(1)} all-to-all(bf16[16,64,128]{2,1,0:T(8,128)(2,1)S(1)} %finish.1), channel_id=1, replica_groups={{0,16,32,48,64,80,96,112,128,144,160,176,192,208,224,240},{8,24,40,56,7..., dimensions={0} | all-to-all | bytes 524288 | tf_op jit(solution)/shard_map/all_to_all | solution.py:60
  94.7 12.9 %collective-permute-start.7 = (bf16[16,64,128]{2,1,0:T(8,128)(2,1)S(1)}, bf16[16,64,128]{2,1,0:T(8,128)(2,1)S(1)}, u32[]{:S(2)}, u32[]{:S(2)}) collective-permute-start(bf16[16,64,128]{2,1,0:T(8,128)(2,1)S(1)} %all_to_all.22.a_ref), channel_id=1, source_target_pairs={{0,8},{8,0},{16,24},{24,16},{32,40},{40,32},{48,56},{56,48},{64,72... | collective-permute-start | bytes 786440 | tf_op jit(solution)/shard_map/ppermute | solution.py:373
  107.6 1.2 %collective-permute-done.7.b_ref = bf16[16,64,128]{2,1,0:T(8,128)(2,1)S(1)} collective-permute-done((bf16[16,64,128]{2,1,0:T(8,128)(2,1)S(1)}, bf16[16,64,128]{2,1,0:T(8,128)(2,1)S(1)}, u32[]{:S(2)}, u32[]{:S(2)}) %collective-permute-start.7) | collective-permute-done | bytes 262176 | tf_op jit(solution)/shard_map/ppermute | solution.py:373
  108.7 0.8 place.1
  (17 shorter events, 0.5 us)
Async XLA Ops:
  0.0 1.0 copy-start.1
  1.1 4.5 %collective-permute-start = (bf16[16,64,128]{2,1,0:T(8,128)(2,1)S(1)}, bf16[16,64,128]{2,1,0:T(8,128)(2,1)S(1)}, u32[]{:S(2)}, u32[]{:S(2)}) collective-permute-start(bf16[16,64,128]{2,1,0:T(8,128)(2,1)S(1)} %get-tuple-element.23), channel_id=1, source_target_pairs={{0,8},{8,0},{16,24},{24,16},{32,40},{40,32},{48,56},{56,48},{64,72... | collective-permute-start | bytes 786440 | tf_op jit(solution)/shard_map/ppermute | solution.py:347
  6.4 13.1 %all-to-all-start = ((bf16[16,64,128]{2,1,0:T(8,128)(2,1)}), bf16[16,64,128]{2,1,0:T(8,128)(2,1)S(1)}, u32[]{:S(2)}, u32[]{:S(2)}) async-start(bf16[16,64,128]{2,1,0:T(8,128)(2,1)} %choose.1), calls=%async_computation | async-start | bytes 524288 | tf_op jit(solution)/shard_map/all_to_all | solution.py:60
  11.4 1.6 %copy-start = (bf16[8192,128]{1,0:T(8,128)(2,1)S(1)}, bf16[8192,128]{1,0:T(8,128)(2,1)}, u32[]{:S(2)}) copy-start(bf16[8192,128]{1,0:T(8,128)(2,1)} %v_ref.1) | copy-start | bytes 6291460
  13.0 0.7 copy-start.2
  30.1 6.9 %collective-permute-start.1 = (bf16[8,64,128]{2,1,0:T(8,128)(2,1)S(1)}, bf16[8,64,128]{2,1,0:T(8,128)(2,1)S(1)}, u32[]{:S(2)}, u32[]{:S(2)}) collective-permute-start(bf16[8,64,128]{2,1,0:T(8,128)(2,1)S(1)} %all_to_all.20), channel_id=1, source_target_pairs={{0,8},{8,0},{16,24},{24,16},{32,40},{40,32},{48,56},{56,48},{64,72... | collective-permute-start | bytes 393224 | tf_op jit(solution)/shard_map/ppermute | solution.py:354
  32.5 5.0 %collective-permute-start.2 = (bf16[8,64,128]{2,1,0:T(8,128)(2,1)S(1)}, bf16[8,64,128]{2,1,0:T(8,128)(2,1)S(1)}, u32[]{:S(2)}, u32[]{:S(2)}) collective-permute-start(bf16[8,64,128]{2,1,0:T(8,128)(2,1)S(1)} %all_to_all.20), channel_id=1, source_target_pairs={{0,16},{8,56},{16,0},{24,40},{32,48},{40,24},{48,32},{56,8},{64,80... | collective-permute-start | bytes 393224 | tf_op jit(solution)/shard_map/ppermute | solution.py:355
  37.5 4.4 %collective-permute-start.3 = (f32[8,72,128]{2,1,0:T(8,128)S(1)}, f32[8,72,128]{2,1,0:T(8,128)S(1)}, u32[]{:S(2)}, u32[]{:S(2)}) collective-permute-start(f32[8,72,128]{2,1,0:T(8,128)S(1)} %get-tuple-element.34), channel_id=1, source_target_pairs={{0,8},{8,0},{16,24},{24,16},{32,40},{40,32},{48,56},{56,48},{64,72... | collective-permute-start | bytes 884744 | tf_op jit(solution)/shard_map/ppermute | solution.py:360
  37.5 4.4 %collective-permute-start.4 = (bf16[8,64,128]{2,1,0:T(8,128)(2,1)S(1)}, bf16[8,64,128]{2,1,0:T(8,128)(2,1)S(1)}, u32[]{:S(2)}, u32[]{:S(2)}) collective-permute-start(bf16[8,64,128]{2,1,0:T(8,128)(2,1)S(1)} %collective-permute-done.2), channel_id=1, source_target_pairs={{0,8},{8,0},{16,24},{24,16},{32,40},{40,32},{48,56},{56,48},{64,72... | collective-permute-start | bytes 393224 | tf_op jit(solution)/shard_map/ppermute | solution.py:361
  42.0 29.9 %collective-permute-start.6 = (f32[8,72,128]{2,1,0:T(8,128)S(1)}, f32[8,72,128]{2,1,0:T(8,128)S(1)}, u32[]{:S(2)}, u32[]{:S(2)}) collective-permute-start(f32[8,72,128]{2,1,0:T(8,128)S(1)} %merge.3), channel_id=1, source_target_pairs={{8,16},{0,56},{24,0},{16,40},{40,48},{32,24},{56,32},{48,8},{72,80... | collective-permute-start | bytes 884744 | tf_op jit(solution)/shard_map/ppermute | solution.py:365
  68.1 3.8 %collective-permute-start.5 = (f32[8,72,128]{2,1,0:T(8,128)S(1)}, f32[8,72,128]{2,1,0:T(8,128)S(1)}, u32[]{:S(2)}, u32[]{:S(2)}) collective-permute-start(f32[8,72,128]{2,1,0:T(8,128)S(1)} %attention.4), channel_id=1, source_target_pairs={{0,8},{8,0},{16,24},{24,16},{32,40},{40,32},{48,56},{56,48},{64,72... | collective-permute-start | bytes 884744 | tf_op jit(solution)/shard_map/ppermute | solution.py:367
  94.7 14.0 %collective-permute-start.7 = (bf16[16,64,128]{2,1,0:T(8,128)(2,1)S(1)}, bf16[16,64,128]{2,1,0:T(8,128)(2,1)S(1)}, u32[]{:S(2)}, u32[]{:S(2)}) collective-permute-start(bf16[16,64,128]{2,1,0:T(8,128)(2,1)S(1)} %all_to_all.22.a_ref), channel_id=1, source_target_pairs={{0,8},{8,0},{16,24},{24,16},{32,40},{40,32},{48,56},{56,48},{64,72... | collective-permute-start | bytes 786440 | tf_op jit(solution)/shard_map/ppermute | solution.py:373

commit v3 on v2

--- a/solution.py
+++ b/solution.py
@@ -40,16 +40,18 @@
 EVERY = [(y, x, core) for y in range(COLUMNS) for x in range(COLUMNS) for core in range(2)]
 PAIR = [(device(*place), partner(*place)) for place in EVERY]
 CROSS = [(device(y, x, 1 - core), partner(y, x, core)) for y, x, core in EVERY]
+COLUMNS_OF = (((0, 3), (1, 2)), ((0, 1), (2, 3)))
 TEAMS = [
-    [device(y, x, core) for y in range(COLUMNS) for x in (side, side + 2)]
+    [device(y, x, core) for y in range(COLUMNS) for x in columns]
     for core in range(2)
-    for side in range(2)
+    for columns in COLUMNS_OF[core]
 ]
 
 
-def member(chip):
+def member(chip, core):
     y, x = divmod(chip, COLUMNS)
-    return x % 2, 2 * y + x // 2
+    team = 0 if x in COLUMNS_OF[core][0] else 1
+    return team, 2 * y + COLUMNS_OF[core][team].index(x)
 
 
 def vmem(limit):
@@ -60,43 +62,54 @@
     return lax.all_to_all(pieces, AXIS, 0, 0, axis_index_groups=groups, tiled=True)
 
 
-def values_kernel(len_ref, k_ref, v_ref, head_ref, o_ref):
-    size = v_ref.shape[0]
-
-    @pl.when(pl.program_id(0) == 0)
-    def _():
-        head_ref[...] = k_ref[...]
-
+def in_hbm(array):
+    return pltpu.with_memory_space_constraint(array, pltpu.HBM)
+
+
+def values_kernel(len_ref, k_ref, v_ref, head_ref, o_ref, held_ref, sems):
+    spans = [slice(start, start + CHUNK) for start in range(0, v_ref.shape[0], CHUNK)]
+    copies = [
+        pltpu.make_async_copy(v_ref.at[span], held_ref.at[span], sems.at[i])
+        for i, span in enumerate(spans)
+    ]
+    copies.append(pltpu.make_async_copy(k_ref.at[spans[0]], head_ref, sems.at[len(spans)]))
+    for copy in copies:
+        copy.start()
     lanes = lax.broadcasted_iota(jnp.int32, (HEAD, HEAD), 1)
     eye = (lanes == lax.broadcasted_iota(jnp.int32, (HEAD, HEAD), 0)).astype(BF16)
-    turned = lax.dot_general(eye, v_ref[...], NT, preferred_element_type=F32)
-    column = pl.program_id(0) * size + lax.broadcasted_iota(jnp.int32, (1, size), 1)
-    valid = column < len_ref[lax.axis_index(AXIS)]
-    o_ref[:HEAD, :] = jnp.where(valid, turned, 0.0).astype(BF16)
-    o_ref[HEAD:, :] = jnp.broadcast_to(jnp.where(valid, 1.0, 0.0), (16, size)).astype(BF16)
+    valid_len = len_ref[lax.axis_index(AXIS)]
+    for copy, span in zip(copies, spans):
+        copy.wait()
+        turned = lax.dot_general(eye, held_ref[span, :], NT, preferred_element_type=F32)
+        valid = span.start + lax.broadcasted_iota(jnp.int32, (1, CHUNK), 1) < valid_len
+        o_ref[:HEAD, span] = jnp.where(valid, turned, 0.0).astype(BF16)
+        ones = jnp.broadcast_to(jnp.where(valid, 1.0, 0.0), (VROWS - HEAD, CHUNK))
+        o_ref[HEAD:, span] = ones.astype(BF16)
+    copies[-1].wait()
 
 
 def turned_values(lengths, keys, values):
     count = values.shape[0]
-    head = pl.BlockSpec((CHUNK, HEAD), lambda i, n: (0, 0))
+    hbm_spec = pl.BlockSpec(memory_space=pltpu.HBM)
+    vmem_spec = pl.BlockSpec(memory_space=pltpu.VMEM)
     return pl.pallas_call(
         values_kernel,
         out_shape=(
             jax.ShapeDtypeStruct((CHUNK, HEAD), BF16),
             jax.ShapeDtypeStruct((VROWS, count), BF16),
         ),
-        grid_spec=pltpu.PrefetchScalarGridSpec(
-            num_scalar_prefetch=1,
-            grid=(count // CHUNK,),
-            in_specs=[head, pl.BlockSpec((CHUNK, HEAD), lambda i, n: (i, 0))],
-            out_specs=(head, pl.BlockSpec((VROWS, CHUNK), lambda i, n: (0, i))),
-        ),
+        in_specs=[pl.BlockSpec(memory_space=pltpu.SMEM), hbm_spec, hbm_spec],
+        out_specs=(vmem_spec, vmem_spec),
+        scratch_shapes=[
+            pltpu.VMEM(values.shape, BF16),
+            pltpu.SemaphoreType.DMA((count // CHUNK + 1,)),
+        ],
         compiler_params=vmem(16),
         cost_estimate=pl.CostEstimate(
             flops=4 * count * HEAD * HEAD, bytes_accessed=5 * count * HEAD, transcendentals=0
         ),
         name="turn_values",
-    )(lengths, pltpu.with_memory_space_constraint(keys, pltpu.HBM), values)
+    )(lengths, in_hbm(keys), in_hbm(values))
 
 
 def write_block(o_ref, out, sums, top):
@@ -118,7 +131,7 @@
 def settle(total, q, k_ref, v_ref, o_ref, acc_ref):
     sums = total[HEAD : HEAD + 1, :]
     write_block(o_ref, total[:HEAD], sums, jnp.zeros_like(sums))
-    good = (sums >= 1.0) & (sums <= 2.0**20)
+    good = (sums >= 2.0**-10) & (sums <= 2.0**20)
     bad = jnp.max(jnp.where(jnp.abs(total[:HEAD]) < 3e38, 0.0, 1.0), axis=0, keepdims=True)
     fine = jnp.max(jnp.where(good, bad, 1.0)) < 0.5
 
@@ -184,7 +197,7 @@
             flops=BLOCK * keys.size // 2, bytes_accessed=keys.size, transcendentals=0
         ),
         name="first_attention",
-    )(rows.reshape(BLOCK, HEAD), head, pltpu.with_memory_space_constraint(keys, pltpu.HBM), values)
+    )(rows.reshape(BLOCK, HEAD), head, in_hbm(keys), values)
 
 
 def attention(rows, keys, values):
@@ -223,37 +236,42 @@
     )(*parts)
 
 
-def split_kernel(q_ref, keep_ref, send_ref):
+def split_kernel(q_ref, keep_ref, send_ref, sems):
     half = q_ref.shape[1] // 2
 
-    def put(ref, start):
+    def put(ref, core, sem):
+        copies = []
         for chip in range(CHIPS):
-            side, place = member(chip)
-            head, part = divmod((1 - side) * PIECES + place, 2)
-            column = start + head * HEAD
-            ref[chip] = q_ref[part * PIECE : (part + 1) * PIECE, column : column + HEAD]
-
-    core = lax.axis_index(AXIS) % 2
-
-    @pl.when(core == 0)
-    def _():
-        put(keep_ref, 0)
-        put(send_ref, half)
-
-    @pl.when(core == 1)
-    def _():
-        put(keep_ref, half)
-        put(send_ref, 0)
+            team, place = member(chip, core)
+            head, part = divmod((1 - team) * PIECES + place, 2)
+            column = core * half + head * HEAD
+            piece = q_ref.at[part * PIECE : (part + 1) * PIECE, column : column + HEAD]
+            copies.append(pltpu.make_async_copy(piece, ref.at[chip], sem.at[chip]))
+        return copies
+
+    for core in range(2):
+
+        @pl.when(lax.axis_index(AXIS) % 2 == core)
+        def _():
+            copies = put(send_ref, 1 - core, sems.at[0]) + put(keep_ref, core, sems.at[1])
+            for copy in copies:
+                copy.start()
+            for copy in copies:
+                copy.wait()
 
 
 def split(block):
     shape = jax.ShapeDtypeStruct((CHIPS, PIECE, HEAD), BF16)
+    vmem_spec = pl.BlockSpec(memory_space=pltpu.VMEM)
     return pl.pallas_call(
         split_kernel,
         out_shape=(shape, shape),
+        in_specs=[pl.BlockSpec(memory_space=pltpu.HBM)],
+        out_specs=(vmem_spec, vmem_spec),
+        scratch_shapes=[pltpu.SemaphoreType.DMA((2, CHIPS))],
         compiler_params=vmem(16),
         name="split",
-    )(block)
+    )(in_hbm(block))
 
 
 def choose_kernel(owner_ref, a_ref, b_ref, o_ref):
@@ -310,14 +328,14 @@
     def _():
         o_ref[...] = jnp.zeros_like(o_ref)
 
-    def put(first, second):
-        for i, ref in enumerate((first, second)):
-            for chip in range(0, CHIPS):
-                side, spot = member(chip)
-                if spot % 2 == 0:
-                    head = (side * PIECES + spot) // 2
-                    block = jnp.concatenate([ref[chip], ref[chip + 2]], axis=0)
-                    o_ref[:, i * half + head * HEAD : i * half + (head + 1) * HEAD] = block.T
+    def put(*halves):
+        for core, ref in enumerate(halves):
+            for team in range(2):
+                left, right = COLUMNS_OF[core][team]
+                for y in range(COLUMNS):
+                    pieces = [ref[y * COLUMNS + x] for x in (left, right)]
+                    column = core * half + (team * COLUMNS + y) * HEAD
+                    o_ref[:, column : column + HEAD] = jnp.concatenate(pieces, axis=0).T
 
     @pl.when(wanted & (me % 2 == 0))
     def _():

time: 110 us -> 108 us (0.982)
  blocking collectives: 33.2 us -> 28.7 us
  starting transfers between devices: 36.2 us -> 39.1 us
  local copies, waits for them, and re-layouts: 3.31 us -> 0.67 us
  waiting for transfers between devices: 4.94 us -> 6.43 us
    all_to_all x3, blocking collectives: 33.2 us -> 28.7 us  [exchange(): lax.all_to_all(pieces, AXIS, 0, 0, axis_index_groups=groups, tiled=True)]
    unnamed x6 -> x2, local copies, waits for them, and re-layouts: 3.28 us -> 0.65 us
    all_to_all x1, waiting for transfers between devices: 2.81 us -> 4.58 us  [exchange(): lax.all_to_all(pieces, AXIS, 0, 0, axis_index_groups=groups, tiled=True)]
    ppermute x1, starting transfers between devices: 2.36 us -> 4.12 us  [per_device(): other_away = lax.ppermute(own_away, AXIS, SWAP)]
    pallas_call x1, Pallas kernels: 0.09 us -> 1.28 us  [split(): pl.pallas_call(split_kernel, out_shape=(shape, shape), in_specs=[pl.Block...]
where the time goes in v3:
time: 108 us
  starting transfers between devices  39.1 us (36%)
  Pallas kernels  31.9 us (30%)
  blocking collectives  28.7 us (27%)
  waiting for transfers between devices  6.43 us (6%)
    all_to_all x3, blocking collectives, exchange(): lax.all_to_all(pieces, AXIS, 0, 0, axis_index_groups=groups, tiled=True)  28.7 us
    pallas_call x3, Pallas kernels, attention(): pl.pallas_call(attention_kernel, out_shape=jax.ShapeDtypeStruct((PIECES,...  21.6 us
    ppermute x1, starting transfers between devices, per_device(): out = place(span_owner, result, lax.ppermute(result, AXIS, SWAP))  13.5 us
    ppermute x1, starting transfers between devices, per_device(): here = lax.ppermute(away, AXIS, CROSS)  11.8 us
    all_to_all x1, starting transfers between devices, exchange(): lax.all_to_all(pieces, AXIS, 0, 0, axis_index_groups=groups, tiled=True)  5.02 us
    all_to_all x1, waiting for transfers between devices, exchange(): lax.all_to_all(pieces, AXIS, 0, 0, axis_index_groups=groups, tiled=True)  4.58 us
    pallas_call x1, Pallas kernels, first_attention(): pl.pallas_call(first_attention_kernel, out_shape=(jax.ShapeDtypeStruct((P...  4.38 us
    ppermute x1, starting transfers between devices, per_device(): other_away = lax.ppermute(own_away, AXIS, SWAP)  4.12 us
  transfers between devices with their start and end apart: 9, of which 4 were waited for; matrix products, arithmetic and copies ran while one was open for 0% of the time, Pallas kernels for 27%

profile of v3, /device:TPU:1, one launch (start us, length us, event | category | flops | bytes accessed | tf_op | source)
XLA Modules:
  0.0 107.6 jit_solution(15331983217663902106)
XLA Ops:
  0.0 1.3 %split.1 = (bf16[16,64,128]{2,1,0:T(8,128)(2,1)S(1)}, bf16[16,64,128]{2,1,0:T(8,128)(2,1)S(1)}) custom-call(bf16[128,2048]{1,0:T(8,128)(2,1)} %bitcast.17), custom_call_target="tpu_custom_call" | custom-call | tf_op jit(solution)/shard_map/split/pallas_call | solution.py:266
  1.3 3.3 %collective-permute-start = (bf16[16,64,128]{2,1,0:T(8,128)(2,1)S(1)}, bf16[16,64,128]{2,1,0:T(8,128)(2,1)S(1)}, u32[]{:S(2)}, u32[]{:S(2)}) collective-permute-start(bf16[16,64,128]{2,1,0:T(8,128)(2,1)S(1)} %get-tuple-element.23), channel_id=1, source_target_pairs={{0,8},{8,0},{16,24},{24,16},{32,40},{40,32},{48,56},{56,48},{64,72... | collective-permute-start | bytes 786440 | tf_op jit(solution)/shard_map/ppermute | solution.py:365
  5.3 0.5 collective-permute-done.b_ref
  5.8 0.7 choose.1
  6.5 5.0 %all-to-all-start = ((bf16[16,64,128]{2,1,0:T(8,128)(2,1)}), bf16[16,64,128]{2,1,0:T(8,128)(2,1)S(1)}, u32[]{:S(2)}, u32[]{:S(2)}) async-start(bf16[16,64,128]{2,1,0:T(8,128)(2,1)} %choose.1), calls=%async_computation | async-start | bytes 524288 | tf_op jit(solution)/shard_map/all_to_all | solution.py:62
  11.6 0.6 copy-done
  12.2 2.8 %turn_values.1 = (bf16[2048,128]{1,0:T(8,128)(2,1)S(1)}, bf16[144,8192]{1,0:T(8,128)(2,1)S(1)}) custom-call(s32[32]{0:T(128)S(1)} %copy-done, bf16[8192,128]{1,0:T(8,128)(2,1)} %k_ref.3, bf16[8192,128]{1,0:T(8,128)(2,1)} %v_ref.1), custom_call_target="tpu_custom_call" | custom-call | flops 536870912 | bytes 5242880 | tf_op jit(solution)/shard_map/turn_values/pallas_call | solution.py:95
  15.1 4.6 %all-to-all-done = bf16[16,64,128]{2,1,0:T(8,128)(2,1)S(1)} async-done(((bf16[16,64,128]{2,1,0:T(8,128)(2,1)}), bf16[16,64,128]{2,1,0:T(8,128)(2,1)S(1)}, u32[]{:S(2)}, u32[]{:S(2)}) %all-to-all-start) | async-done | bytes 262176 | tf_op jit(solution)/shard_map/all_to_all | solution.py:62
  19.7 7.9 %all_to_all.20 = bf16[8,64,128]{2,1,0:T(8,128)(2,1)S(1)} all-to-all(bf16[8,64,128]{2,1,0:T(8,128)(2,1)S(1)} %broadcast_in_dim.4), channel_id=1, replica_groups={{0,48,64,112,128,176,192,240},{16,32,80,96,144,160,208,224},{8,24,72,88..., dimensions={0} | all-to-all | bytes 262144 | tf_op jit(solution)/shard_map/all_to_all | solution.py:62
  27.6 4.1 %collective-permute-start.1 = (bf16[8,64,128]{2,1,0:T(8,128)(2,1)S(1)}, bf16[8,64,128]{2,1,0:T(8,128)(2,1)S(1)}, u32[]{:S(2)}, u32[]{:S(2)}) collective-permute-start(bf16[8,64,128]{2,1,0:T(8,128)(2,1)S(1)} %all_to_all.20), channel_id=1, source_target_pairs={{0,8},{8,0},{16,24},{24,16},{32,40},{40,32},{48,56},{56,48},{64,72... | collective-permute-start | bytes 393224 | tf_op jit(solution)/shard_map/ppermute | solution.py:372
  31.7 0.5 collective-permute-start.2
  32.2 4.4 %first_attention.1 = (f32[8,72,128]{2,1,0:T(8,128)S(1)}, bf16[8192,128]{1,0:T(8,128)(2,1)S(1)}) custom-call(bf16[512,128]{1,0:T(8,128)(2,1)S(1)} %bitcast.13, bf16[2048,128]{1,0:T(8,128)(2,1)S(1)} %get-tuple-element.29.head_ref, bf16[8192,128]{1,0:T(8,128)(2,1)} %k_ref.3, bf16[144,8192]{1,0:T(8,128)(2,1)S(1)} %get-tuple-element.30.v_ref), custom_call_target="tpu_custom_call" | custom-call | flops 268435456 | bytes 1048576 | tf_op jit(solution)/shard_map/first_attention/pallas_call | solution.py:183
  36.6 0.2 collective-permute-done.2
  36.7 0.5 collective-permute-start.4
  37.3 3.7 %attention.3.refs_0_ = f32[8,72,128]{2,1,0:T(8,128)S(1)} custom-call(bf16[512,128]{1,0:T(8,128)(2,1)S(1)} %bitcast.15, bf16[8192,128]{1,0:T(8,128)(2,1)S(1)} %get-tuple-element.33.k_ref, bf16[144,8192]{1,0:T(8,128)(2,1)S(1)} %get-tuple-element.30.v_ref), custom_call_target="tpu_custom_call" | custom-call | flops 268435456 | bytes 1048576 | tf_op jit(solution)/shard_map/attention/pallas_call | solution.py:205
  41.0 11.8 %collective-permute-start.6 = (f32[8,72,128]{2,1,0:T(8,128)S(1)}, f32[8,72,128]{2,1,0:T(8,128)S(1)}, u32[]{:S(2)}, u32[]{:S(2)}) collective-permute-start(f32[8,72,128]{2,1,0:T(8,128)S(1)} %merge.3), channel_id=1, source_target_pairs={{8,16},{0,56},{24,0},{16,40},{40,48},{32,24},{56,32},{48,8},{72,80... | collective-permute-start | bytes 884744 | tf_op jit(solution)/shard_map/ppermute | solution.py:383
  52.8 14.3 %attention.4 = f32[8,72,128]{2,1,0:T(8,128)S(1)} custom-call(bf16[512,128]{1,0:T(8,128)(2,1)S(1)} %bitcast.16, bf16[8192,128]{1,0:T(8,128)(2,1)S(1)} %get-tuple-element.33.k_ref, bf16[144,8192]{1,0:T(8,128)(2,1)S(1)} %get-tuple-element.30.v_ref), custom_call_target="tpu_custom_call" | custom-call | flops 268435456 | bytes 1048576 | tf_op jit(solution)/shard_map/attention/pallas_call | solution.py:205
  67.1 0.3 collective-permute-start.5
  67.5 3.7 %attention.5.refs_0_ = f32[8,72,128]{2,1,0:T(8,128)S(1)} custom-call(bf16[512,128]{1,0:T(8,128)(2,1)S(1)} %bitcast.14, bf16[8192,128]{1,0:T(8,128)(2,1)S(1)} %get-tuple-element.33.k_ref, bf16[144,8192]{1,0:T(8,128)(2,1)S(1)} %get-tuple-element.30.v_ref), custom_call_target="tpu_custom_call" | custom-call | flops 268435456 | bytes 1048576 | tf_op jit(solution)/shard_map/attention/pallas_call | solution.py:205
  71.3 8.9 %all_to_all.21.r_ref = f32[8,72,128]{2,1,0:T(8,128)S(1)} all-to-all(f32[8,72,128]{2,1,0:T(8,128)S(1)} %merge.5), channel_id=1, replica_groups={{0,48,64,112,128,176,192,240},{16,32,80,96,144,160,208,224},{8,24,72,88..., dimensions={0} | all-to-all | bytes 589824 | tf_op jit(solution)/shard_map/all_to_all | solution.py:62
  80.2 11.8 %all_to_all.22.a_ref = bf16[16,64,128]{2,1,0:T(8,128)(2,1)S(1)} all-to-all(bf16[16,64,128]{2,1,0:T(8,128)(2,1)S(1)} %finish.1), channel_id=1, replica_groups={{0,16,32,48,64,80,96,112,128,144,160,176,192,208,224,240},{8,24,40,56,7..., dimensions={0} | all-to-all | bytes 524288 | tf_op jit(solution)/shard_map/all_to_all | solution.py:62
  92.1 13.5 %collective-permute-start.7 = (bf16[16,64,128]{2,1,0:T(8,128)(2,1)S(1)}, bf16[16,64,128]{2,1,0:T(8,128)(2,1)S(1)}, u32[]{:S(2)}, u32[]{:S(2)}) collective-permute-start(bf16[16,64,128]{2,1,0:T(8,128)(2,1)S(1)} %all_to_all.22.a_ref), channel_id=1, source_target_pairs={{0,8},{8,0},{16,24},{24,16},{32,40},{40,32},{48,56},{56,48},{64,72... | collective-permute-start | bytes 786440 | tf_op jit(solution)/shard_map/ppermute | solution.py:391
  105.6 1.2 %collective-permute-done.7.b_ref = bf16[16,64,128]{2,1,0:T(8,128)(2,1)S(1)} collective-permute-done((bf16[16,64,128]{2,1,0:T(8,128)(2,1)S(1)}, bf16[16,64,128]{2,1,0:T(8,128)(2,1)S(1)}, u32[]{:S(2)}, u32[]{:S(2)}) %collective-permute-start.7) | collective-permute-done | bytes 262176 | tf_op jit(solution)/shard_map/ppermute | solution.py:391
  106.7 0.8 place.1
  (13 shorter events, 0.2 us)
Async XLA Ops:
  1.3 4.5 %collective-permute-start = (bf16[16,64,128]{2,1,0:T(8,128)(2,1)S(1)}, bf16[16,64,128]{2,1,0:T(8,128)(2,1)S(1)}, u32[]{:S(2)}, u32[]{:S(2)}) collective-permute-start(bf16[16,64,128]{2,1,0:T(8,128)(2,1)S(1)} %get-tuple-element.23), channel_id=1, source_target_pairs={{0,8},{8,0},{16,24},{24,16},{32,40},{40,32},{48,56},{56,48},{64,72... | collective-permute-start | bytes 786440 | tf_op jit(solution)/shard_map/ppermute | solution.py:365
  6.5 13.1 %all-to-all-start = ((bf16[16,64,128]{2,1,0:T(8,128)(2,1)}), bf16[16,64,128]{2,1,0:T(8,128)(2,1)S(1)}, u32[]{:S(2)}, u32[]{:S(2)}) async-start(bf16[16,64,128]{2,1,0:T(8,128)(2,1)} %choose.1), calls=%async_computation | async-start | bytes 524288 | tf_op jit(solution)/shard_map/all_to_all | solution.py:62
  11.6 0.7 copy-start
  27.6 9.0 %collective-permute-start.1 = (bf16[8,64,128]{2,1,0:T(8,128)(2,1)S(1)}, bf16[8,64,128]{2,1,0:T(8,128)(2,1)S(1)}, u32[]{:S(2)}, u32[]{:S(2)}) collective-permute-start(bf16[8,64,128]{2,1,0:T(8,128)(2,1)S(1)} %all_to_all.20), channel_id=1, source_target_pairs={{0,8},{8,0},{16,24},{24,16},{32,40},{40,32},{48,56},{56,48},{64,72... | collective-permute-start | bytes 393224 | tf_op jit(solution)/shard_map/ppermute | solution.py:372
  31.7 5.0 %collective-permute-start.2 = (bf16[8,64,128]{2,1,0:T(8,128)(2,1)S(1)}, bf16[8,64,128]{2,1,0:T(8,128)(2,1)S(1)}, u32[]{:S(2)}, u32[]{:S(2)}) collective-permute-start(bf16[8,64,128]{2,1,0:T(8,128)(2,1)S(1)} %all_to_all.20), channel_id=1, source_target_pairs={{0,16},{8,56},{16,0},{24,40},{32,48},{40,24},{48,32},{56,8},{64,80... | collective-permute-start | bytes 393224 | tf_op jit(solution)/shard_map/ppermute | solution.py:373
  36.7 4.2 %collective-permute-start.3 = (f32[8,72,128]{2,1,0:T(8,128)S(1)}, f32[8,72,128]{2,1,0:T(8,128)S(1)}, u32[]{:S(2)}, u32[]{:S(2)}) collective-permute-start(f32[8,72,128]{2,1,0:T(8,128)S(1)} %get-tuple-element.34), channel_id=1, source_target_pairs={{0,8},{8,0},{16,24},{24,16},{32,40},{40,32},{48,56},{56,48},{64,72... | collective-permute-start | bytes 884744 | tf_op jit(solution)/shard_map/ppermute | solution.py:378
  36.7 4.3 %collective-permute-start.4 = (bf16[8,64,128]{2,1,0:T(8,128)(2,1)S(1)}, bf16[8,64,128]{2,1,0:T(8,128)(2,1)S(1)}, u32[]{:S(2)}, u32[]{:S(2)}) collective-permute-start(bf16[8,64,128]{2,1,0:T(8,128)(2,1)S(1)} %collective-permute-done.2), channel_id=1, source_target_pairs={{0,8},{8,0},{16,24},{24,16},{32,40},{40,32},{48,56},{56,48},{64,72... | collective-permute-start | bytes 393224 | tf_op jit(solution)/shard_map/ppermute | solution.py:379
  41.0 30.1 %collective-permute-start.6 = (f32[8,72,128]{2,1,0:T(8,128)S(1)}, f32[8,72,128]{2,1,0:T(8,128)S(1)}, u32[]{:S(2)}, u32[]{:S(2)}) collective-permute-start(f32[8,72,128]{2,1,0:T(8,128)S(1)} %merge.3), channel_id=1, source_target_pairs={{8,16},{0,56},{24,0},{16,40},{40,48},{32,24},{56,32},{48,8},{72,80... | collective-permute-start | bytes 884744 | tf_op jit(solution)/shard_map/ppermute | solution.py:383
  67.1 4.1 %collective-permute-start.5 = (f32[8,72,128]{2,1,0:T(8,128)S(1)}, f32[8,72,128]{2,1,0:T(8,128)S(1)}, u32[]{:S(2)}, u32[]{:S(2)}) collective-permute-start(f32[8,72,128]{2,1,0:T(8,128)S(1)} %attention.4), channel_id=1, source_target_pairs={{0,8},{8,0},{16,24},{24,16},{32,40},{40,32},{48,56},{56,48},{64,72... | collective-permute-start | bytes 884744 | tf_op jit(solution)/shard_map/ppermute | solution.py:385
  92.1 14.7 %collective-permute-start.7 = (bf16[16,64,128]{2,1,0:T(8,128)(2,1)S(1)}, bf16[16,64,128]{2,1,0:T(8,128)(2,1)S(1)}, u32[]{:S(2)}, u32[]{:S(2)}) collective-permute-start(bf16[16,64,128]{2,1,0:T(8,128)(2,1)S(1)} %all_to_all.22.a_ref), channel_id=1, source_target_pairs={{0,8},{8,0},{16,24},{24,16},{32,40},{40,32},{48,56},{56,48},{64,72... | collective-permute-start | bytes 786440 | tf_op jit(solution)/shard_map/ppermute | solution.py:391

commit v4 on v3

--- a/solution.py
+++ b/solution.py
@@ -26,32 +26,41 @@
 NT = (((1,), (1,)), ((), ()))
 
 SWAP = [(i, i ^ 1) for i in range(2 * CHIPS)]
-PLANE = [[2 * chip + core for chip in range(CHIPS)] for core in range(2)]
+
+
+def snake(chip):
+    y, x = divmod(chip, COLUMNS)
+    return y * COLUMNS + (COLUMNS - 1 - x if y % 2 else x)
+
+
+PLANE = [[2 * snake(place) + core for place in range(CHIPS)] for core in range(2)]
 
 
 def device(y, x, core):
-    return (y * COLUMNS + x % COLUMNS) * 2 + core
+    return (y % COLUMNS * COLUMNS + x % COLUMNS) * 2 + core
 
 
 def partner(y, x, core):
-    return device(y, x + (1 if (x + core) % 2 == 0 else -1), core)
+    if core == 0:
+        return device(y + (1 if y % 2 else -1), x, core)
+    return device(y, x + (1 if x % 2 else -1), core)
 
 
 EVERY = [(y, x, core) for y in range(COLUMNS) for x in range(COLUMNS) for core in range(2)]
 PAIR = [(device(*place), partner(*place)) for place in EVERY]
 CROSS = [(device(y, x, 1 - core), partner(y, x, core)) for y, x, core in EVERY]
-COLUMNS_OF = (((0, 3), (1, 2)), ((0, 1), (2, 3)))
-TEAMS = [
-    [device(y, x, core) for y in range(COLUMNS) for x in columns]
-    for core in range(2)
-    for columns in COLUMNS_OF[core]
-]
-
-
 def member(chip, core):
     y, x = divmod(chip, COLUMNS)
-    team = 0 if x in COLUMNS_OF[core][0] else 1
-    return team, 2 * y + COLUMNS_OF[core][team].index(x)
+    short, long = (y, x) if core == 0 else (x, y)
+    return short // 2, 2 * long + short % 2
+
+
+SEATS = [
+    [sorted((c for c in range(CHIPS) if member(c, core)[0] == team), key=lambda c: member(c, core)[1])
+     for team in range(2)]
+    for core in range(2)
+]
+TEAMS = [[2 * chip + core for chip in SEATS[core][team]] for core in range(2) for team in range(2)]
 
 
 def vmem(limit):
@@ -246,7 +255,7 @@
             head, part = divmod((1 - team) * PIECES + place, 2)
             column = core * half + head * HEAD
             piece = q_ref.at[part * PIECE : (part + 1) * PIECE, column : column + HEAD]
-            copies.append(pltpu.make_async_copy(piece, ref.at[chip], sem.at[chip]))
+            copies.append(pltpu.make_async_copy(piece, ref.at[snake(chip)], sem.at[chip]))
         return copies
 
     for core in range(2):
@@ -331,10 +340,10 @@
     def put(*halves):
         for core, ref in enumerate(halves):
             for team in range(2):
-                left, right = COLUMNS_OF[core][team]
-                for y in range(COLUMNS):
-                    pieces = [ref[y * COLUMNS + x] for x in (left, right)]
-                    column = core * half + (team * COLUMNS + y) * HEAD
+                chips = SEATS[core][team]
+                for spot in range(0, PIECES, 2):
+                    pieces = [ref[snake(chip)] for chip in chips[spot : spot + 2]]
+                    column = core * half + (team * PIECES + spot) // 2 * HEAD
                     o_ref[:, column : column + HEAD] = jnp.concatenate(pieces, axis=0).T
 
     @pl.when(wanted & (me % 2 == 0))
@@ -365,7 +374,9 @@
     mine = choose(span_owner, keep, lax.ppermute(send, AXIS, SWAP))
     lengths, mine = lax.optimization_barrier((lengths, mine))
     first_keys, values = turned_values(lengths, cache_keys, cache_values)
-    piece = lax.dynamic_index_in_dim(exchange(mine, PLANE), span_owner[0] // 2, 0, False)
+    y, x = span_owner[0] // (2 * COLUMNS), span_owner[0] // 2 % COLUMNS
+    slot = y * COLUMNS + jnp.where(y % 2 == 1, COLUMNS - 1 - x, x)
+    piece = lax.dynamic_index_in_dim(exchange(mine, PLANE), slot, 0, False)
     piece, first_keys, values = lax.optimization_barrier((piece, first_keys, values))
 
     own_away = exchange(jnp.broadcast_to(piece[None], (PIECES, PIECE, HEAD)), TEAMS)

time: 108 us -> 106 us (0.981)
  starting transfers between devices: 39.1 us -> 37.5 us
  waiting for transfers between devices: 6.43 us -> 5.27 us
    ppermute x1, starting transfers between devices: 13.5 us -> 11.9 us  [per_device(): out = place(span_owner, result, lax.ppermute(result, AXIS, SWAP))]
    ppermute x1, starting transfers between devices: 4.12 us -> 2.94 us  [per_device(): other_away = lax.ppermute(own_away, AXIS, SWAP)]
    all_to_all x1, waiting for transfers between devices: 4.58 us -> 3.49 us  [exchange(): lax.all_to_all(pieces, AXIS, 0, 0, axis_index_groups=groups, tiled=True)]
where the time goes in v4:
time: 106 us
  starting transfers between devices  37.5 us (35%)
  Pallas kernels  31.9 us (30%)
  blocking collectives  29.6 us (28%)
  waiting for transfers between devices  5.27 us (5%)
    all_to_all x3, blocking collectives, exchange(): lax.all_to_all(pieces, AXIS, 0, 0, axis_index_groups=groups, tiled=True)  29.6 us
    pallas_call x3, Pallas kernels, attention(): pl.pallas_call(attention_kernel, out_shape=jax.ShapeDtypeStruct((PIECES,...  21.6 us
    ppermute x1, starting transfers between devices, per_device(): here = lax.ppermute(away, AXIS, CROSS)  12.2 us
    ppermute x1, starting transfers between devices, per_device(): out = place(span_owner, result, lax.ppermute(result, AXIS, SWAP))  11.9 us
    all_to_all x1, starting transfers between devices, exchange(): lax.all_to_all(pieces, AXIS, 0, 0, axis_index_groups=groups, tiled=True)  5.02 us
    pallas_call x1, Pallas kernels, first_attention(): pl.pallas_call(first_attention_kernel, out_shape=(jax.ShapeDtypeStruct((P...  4.38 us
    all_to_all x1, waiting for transfers between devices, exchange(): lax.all_to_all(pieces, AXIS, 0, 0, axis_index_groups=groups, tiled=True)  3.49 us
    ppermute x1, starting transfers between devices, per_device(): mine = choose(span_owner, keep, lax.ppermute(send, AXIS, SWAP))  3.33 us
  transfers between devices with their start and end apart: 9, of which 4 were waited for; matrix products, arithmetic and copies ran while one was open for 0% of the time, Pallas kernels for 27%

profile of v4, /device:TPU:1, one launch (start us, length us, event | category | flops | bytes accessed | tf_op | source)
XLA Modules:
  0.0 105.9 jit_solution(9484651399077048797)
XLA Ops:
  0.0 1.3 %split.1 = (bf16[16,64,128]{2,1,0:T(8,128)(2,1)S(1)}, bf16[16,64,128]{2,1,0:T(8,128)(2,1)S(1)}) custom-call(bf16[128,2048]{1,0:T(8,128)(2,1)} %bitcast.17), custom_call_target="tpu_custom_call" | custom-call | tf_op jit(solution)/shard_map/split/pallas_call | solution.py:275
  1.3 3.3 %collective-permute-start = (bf16[16,64,128]{2,1,0:T(8,128)(2,1)S(1)}, bf16[16,64,128]{2,1,0:T(8,128)(2,1)S(1)}, u32[]{:S(2)}, u32[]{:S(2)}) collective-permute-start(bf16[16,64,128]{2,1,0:T(8,128)(2,1)S(1)} %get-tuple-element.23), channel_id=1, source_target_pairs={{0,8},{8,0},{16,24},{24,16},{32,40},{40,32},{48,56},{56,48},{64,72... | collective-permute-start | bytes 786440 | tf_op jit(solution)/shard_map/ppermute | solution.py:374
  5.3 0.5 collective-permute-done.b_ref
  5.8 0.7 choose.1
  6.5 5.0 %all-to-all-start = ((bf16[16,64,128]{2,1,0:T(8,128)(2,1)}), bf16[16,64,128]{2,1,0:T(8,128)(2,1)S(1)}, u32[]{:S(2)}, u32[]{:S(2)}) async-start(bf16[16,64,128]{2,1,0:T(8,128)(2,1)} %choose.1), calls=%async_computation | async-start | bytes 524288 | tf_op jit(solution)/shard_map/all_to_all | solution.py:71
  11.6 0.6 copy-done
  12.3 2.8 %turn_values.1 = (bf16[2048,128]{1,0:T(8,128)(2,1)S(1)}, bf16[144,8192]{1,0:T(8,128)(2,1)S(1)}) custom-call(s32[32]{0:T(128)S(1)} %copy-done, bf16[8192,128]{1,0:T(8,128)(2,1)} %k_ref.3, bf16[8192,128]{1,0:T(8,128)(2,1)} %v_ref.1), custom_call_target="tpu_custom_call" | custom-call | flops 536870912 | bytes 5242880 | tf_op jit(solution)/shard_map/turn_values/pallas_call | solution.py:104
  15.1 3.5 %all-to-all-done = bf16[16,64,128]{2,1,0:T(8,128)(2,1)S(1)} async-done(((bf16[16,64,128]{2,1,0:T(8,128)(2,1)}), bf16[16,64,128]{2,1,0:T(8,128)(2,1)S(1)}, u32[]{:S(2)}, u32[]{:S(2)}) %all-to-all-start) | async-done | bytes 262176 | tf_op jit(solution)/shard_map/all_to_all | solution.py:71
  18.6 8.2 %all_to_all.20 = bf16[8,64,128]{2,1,0:T(8,128)(2,1)S(1)} all-to-all(bf16[8,64,128]{2,1,0:T(8,128)(2,1)S(1)} %broadcast_in_dim.4), channel_id=1, replica_groups={{0,64,16,80,32,96,48,112},{128,192,144,208,160,224,176,240},{8,24,72,88..., dimensions={0} | all-to-all | bytes 262144 | tf_op jit(solution)/shard_map/all_to_all | solution.py:71
  26.8 2.9 %collective-permute-start.1 = (bf16[8,64,128]{2,1,0:T(8,128)(2,1)S(1)}, bf16[8,64,128]{2,1,0:T(8,128)(2,1)S(1)}, u32[]{:S(2)}, u32[]{:S(2)}) collective-permute-start(bf16[8,64,128]{2,1,0:T(8,128)(2,1)S(1)} %all_to_all.20), channel_id=1, source_target_pairs={{0,8},{8,0},{16,24},{24,16},{32,40},{40,32},{48,56},{56,48},{64,72... | collective-permute-start | bytes 393224 | tf_op jit(solution)/shard_map/ppermute | solution.py:383
  29.8 0.8 collective-permute-start.2
  30.6 4.4 %first_attention.1 = (f32[8,72,128]{2,1,0:T(8,128)S(1)}, bf16[8192,128]{1,0:T(8,128)(2,1)S(1)}) custom-call(bf16[512,128]{1,0:T(8,128)(2,1)S(1)} %bitcast.13, bf16[2048,128]{1,0:T(8,128)(2,1)S(1)} %get-tuple-element.29.head_ref, bf16[8192,128]{1,0:T(8,128)(2,1)} %k_ref.3, bf16[144,8192]{1,0:T(8,128)(2,1)S(1)} %get-tuple-element.30.v_ref), custom_call_target="tpu_custom_call" | custom-call | flops 268435456 | bytes 1048576 | tf_op jit(solution)/shard_map/first_attention/pallas_call | solution.py:192
  35.1 0.9 collective-permute-start.3
  36.0 0.2 collective-permute-start.4
  36.2 3.7 %attention.3.refs_0_ = f32[8,72,128]{2,1,0:T(8,128)S(1)} custom-call(bf16[512,128]{1,0:T(8,128)(2,1)S(1)} %bitcast.15, bf16[8192,128]{1,0:T(8,128)(2,1)S(1)} %get-tuple-element.33.k_ref, bf16[144,8192]{1,0:T(8,128)(2,1)S(1)} %get-tuple-element.30.v_ref), custom_call_target="tpu_custom_call" | custom-call | flops 268435456 | bytes 1048576 | tf_op jit(solution)/shard_map/attention/pallas_call | solution.py:214
  39.9 12.2 %collective-permute-start.6 = (f32[8,72,128]{2,1,0:T(8,128)S(1)}, f32[8,72,128]{2,1,0:T(8,128)S(1)}, u32[]{:S(2)}, u32[]{:S(2)}) collective-permute-start(f32[8,72,128]{2,1,0:T(8,128)S(1)} %merge.3), channel_id=1, source_target_pairs={{8,192},{0,56},{24,208},{16,40},{40,224},{32,24},{56,240},{48,8},{... | collective-permute-start | bytes 884744 | tf_op jit(solution)/shard_map/ppermute | solution.py:394
  52.1 14.3 %attention.4 = f32[8,72,128]{2,1,0:T(8,128)S(1)} custom-call(bf16[512,128]{1,0:T(8,128)(2,1)S(1)} %bitcast.16, bf16[8192,128]{1,0:T(8,128)(2,1)S(1)} %get-tuple-element.33.k_ref, bf16[144,8192]{1,0:T(8,128)(2,1)S(1)} %get-tuple-element.30.v_ref), custom_call_target="tpu_custom_call" | custom-call | flops 268435456 | bytes 1048576 | tf_op jit(solution)/shard_map/attention/pallas_call | solution.py:214
  66.4 0.3 collective-permute-start.5
  66.7 3.7 %attention.5.refs_0_ = f32[8,72,128]{2,1,0:T(8,128)S(1)} custom-call(bf16[512,128]{1,0:T(8,128)(2,1)S(1)} %bitcast.14, bf16[8192,128]{1,0:T(8,128)(2,1)S(1)} %get-tuple-element.33.k_ref, bf16[144,8192]{1,0:T(8,128)(2,1)S(1)} %get-tuple-element.30.v_ref), custom_call_target="tpu_custom_call" | custom-call | flops 268435456 | bytes 1048576 | tf_op jit(solution)/shard_map/attention/pallas_call | solution.py:214
  70.6 9.8 %all_to_all.21.r_ref = f32[8,72,128]{2,1,0:T(8,128)S(1)} all-to-all(f32[8,72,128]{2,1,0:T(8,128)S(1)} %merge.5), channel_id=1, replica_groups={{0,64,16,80,32,96,48,112},{128,192,144,208,160,224,176,240},{8,24,72,88..., dimensions={0} | all-to-all | bytes 589824 | tf_op jit(solution)/shard_map/all_to_all | solution.py:71
  80.5 11.6 %all_to_all.22.a_ref = bf16[16,64,128]{2,1,0:T(8,128)(2,1)S(1)} all-to-all(bf16[16,64,128]{2,1,0:T(8,128)(2,1)S(1)} %finish.1), channel_id=1, replica_groups={{0,16,32,48,112,96,80,64,128,144,160,176,240,224,208,192},{8,24,40,56,1..., dimensions={0} | all-to-all | bytes 524288 | tf_op jit(solution)/shard_map/all_to_all | solution.py:71
  92.0 11.9 %collective-permute-start.7 = (bf16[16,64,128]{2,1,0:T(8,128)(2,1)S(1)}, bf16[16,64,128]{2,1,0:T(8,128)(2,1)S(1)}, u32[]{:S(2)}, u32[]{:S(2)}) collective-permute-start(bf16[16,64,128]{2,1,0:T(8,128)(2,1)S(1)} %all_to_all.22.a_ref), channel_id=1, source_target_pairs={{0,8},{8,0},{16,24},{24,16},{32,40},{40,32},{48,56},{56,48},{64,72... | collective-permute-start | bytes 786440 | tf_op jit(solution)/shard_map/ppermute | solution.py:402
  103.9 1.2 %collective-permute-done.7.b_ref = bf16[16,64,128]{2,1,0:T(8,128)(2,1)S(1)} collective-permute-done((bf16[16,64,128]{2,1,0:T(8,128)(2,1)S(1)}, bf16[16,64,128]{2,1,0:T(8,128)(2,1)S(1)}, u32[]{:S(2)}, u32[]{:S(2)}) %collective-permute-start.7) | collective-permute-done | bytes 262176 | tf_op jit(solution)/shard_map/ppermute | solution.py:402
  105.1 0.8 place.1
  (13 shorter events, 0.3 us)
Async XLA Ops:
  1.3 4.5 %collective-permute-start = (bf16[16,64,128]{2,1,0:T(8,128)(2,1)S(1)}, bf16[16,64,128]{2,1,0:T(8,128)(2,1)S(1)}, u32[]{:S(2)}, u32[]{:S(2)}) collective-permute-start(bf16[16,64,128]{2,1,0:T(8,128)(2,1)S(1)} %get-tuple-element.23), channel_id=1, source_target_pairs={{0,8},{8,0},{16,24},{24,16},{32,40},{40,32},{48,56},{56,48},{64,72... | collective-permute-start | bytes 786440 | tf_op jit(solution)/shard_map/ppermute | solution.py:374
  6.5 12.1 %all-to-all-start = ((bf16[16,64,128]{2,1,0:T(8,128)(2,1)}), bf16[16,64,128]{2,1,0:T(8,128)(2,1)S(1)}, u32[]{:S(2)}, u32[]{:S(2)}) async-start(bf16[16,64,128]{2,1,0:T(8,128)(2,1)} %choose.1), calls=%async_computation | async-start | bytes 524288 | tf_op jit(solution)/shard_map/all_to_all | solution.py:71
  11.6 0.7 copy-start
  26.8 8.2 %collective-permute-start.1 = (bf16[8,64,128]{2,1,0:T(8,128)(2,1)S(1)}, bf16[8,64,128]{2,1,0:T(8,128)(2,1)S(1)}, u32[]{:S(2)}, u32[]{:S(2)}) collective-permute-start(bf16[8,64,128]{2,1,0:T(8,128)(2,1)S(1)} %all_to_all.20), channel_id=1, source_target_pairs={{0,8},{8,0},{16,24},{24,16},{32,40},{40,32},{48,56},{56,48},{64,72... | collective-permute-start | bytes 393224 | tf_op jit(solution)/shard_map/ppermute | solution.py:383
  29.8 5.3 %collective-permute-start.2 = (bf16[8,64,128]{2,1,0:T(8,128)(2,1)S(1)}, bf16[8,64,128]{2,1,0:T(8,128)(2,1)S(1)}, u32[]{:S(2)}, u32[]{:S(2)}) collective-permute-start(bf16[8,64,128]{2,1,0:T(8,128)(2,1)S(1)} %all_to_all.20), channel_id=1, source_target_pairs={{0,192},{8,56},{16,208},{24,40},{32,224},{40,24},{48,240},{56,8},{... | collective-permute-start | bytes 393224 | tf_op jit(solution)/shard_map/ppermute | solution.py:384
  35.1 4.8 %collective-permute-start.3 = (f32[8,72,128]{2,1,0:T(8,128)S(1)}, f32[8,72,128]{2,1,0:T(8,128)S(1)}, u32[]{:S(2)}, u32[]{:S(2)}) collective-permute-start(f32[8,72,128]{2,1,0:T(8,128)S(1)} %get-tuple-element.34), channel_id=1, source_target_pairs={{0,8},{8,0},{16,24},{24,16},{32,40},{40,32},{48,56},{56,48},{64,72... | collective-permute-start | bytes 884744 | tf_op jit(solution)/shard_map/ppermute | solution.py:389
  36.0 4.0 %collective-permute-start.4 = (bf16[8,64,128]{2,1,0:T(8,128)(2,1)S(1)}, bf16[8,64,128]{2,1,0:T(8,128)(2,1)S(1)}, u32[]{:S(2)}, u32[]{:S(2)}) collective-permute-start(bf16[8,64,128]{2,1,0:T(8,128)(2,1)S(1)} %collective-permute-done.2), channel_id=1, source_target_pairs={{0,8},{8,0},{16,24},{24,16},{32,40},{40,32},{48,56},{56,48},{64,72... | collective-permute-start | bytes 393224 | tf_op jit(solution)/shard_map/ppermute | solution.py:390
  39.9 30.5 %collective-permute-start.6 = (f32[8,72,128]{2,1,0:T(8,128)S(1)}, f32[8,72,128]{2,1,0:T(8,128)S(1)}, u32[]{:S(2)}, u32[]{:S(2)}) collective-permute-start(f32[8,72,128]{2,1,0:T(8,128)S(1)} %merge.3), channel_id=1, source_target_pairs={{8,192},{0,56},{24,208},{16,40},{40,224},{32,24},{56,240},{48,8},{... | collective-permute-start | bytes 884744 | tf_op jit(solution)/shard_map/ppermute | solution.py:394
  66.4 4.1 %collective-permute-start.5 = (f32[8,72,128]{2,1,0:T(8,128)S(1)}, f32[8,72,128]{2,1,0:T(8,128)S(1)}, u32[]{:S(2)}, u32[]{:S(2)}) collective-permute-start(f32[8,72,128]{2,1,0:T(8,128)S(1)} %attention.4), channel_id=1, source_target_pairs={{0,8},{8,0},{16,24},{24,16},{32,40},{40,32},{48,56},{56,48},{64,72... | collective-permute-start | bytes 884744 | tf_op jit(solution)/shard_map/ppermute | solution.py:396
  92.0 13.0 %collective-permute-start.7 = (bf16[16,64,128]{2,1,0:T(8,128)(2,1)S(1)}, bf16[16,64,128]{2,1,0:T(8,128)(2,1)S(1)}, u32[]{:S(2)}, u32[]{:S(2)}) collective-permute-start(bf16[16,64,128]{2,1,0:T(8,128)(2,1)S(1)} %all_to_all.22.a_ref), channel_id=1, source_target_pairs={{0,8},{8,0},{16,24},{24,16},{32,40},{40,32},{48,56},{56,48},{64,72... | collective-permute-start | bytes 786440 | tf_op jit(solution)/shard_map/ppermute | solution.py:402

commit v5 on v4

--- a/solution.py
+++ b/solution.py
@@ -75,7 +75,7 @@
     return pltpu.with_memory_space_constraint(array, pltpu.HBM)
 
 
-def values_kernel(len_ref, k_ref, v_ref, head_ref, o_ref, held_ref, sems):
+def values_kernel(len_ref, k_ref, v_ref, head_ref, o_ref, blank_ref, held_ref, zero_ref, sems):
     spans = [slice(start, start + CHUNK) for start in range(0, v_ref.shape[0], CHUNK)]
     copies = [
         pltpu.make_async_copy(v_ref.at[span], held_ref.at[span], sems.at[i])
@@ -84,6 +84,9 @@
     copies.append(pltpu.make_async_copy(k_ref.at[spans[0]], head_ref, sems.at[len(spans)]))
     for copy in copies:
         copy.start()
+    zero_ref[...] = jnp.zeros_like(zero_ref)
+    blank = pltpu.make_async_copy(zero_ref, blank_ref, sems.at[len(spans) + 1])
+    blank.start()
     lanes = lax.broadcasted_iota(jnp.int32, (HEAD, HEAD), 1)
     eye = (lanes == lax.broadcasted_iota(jnp.int32, (HEAD, HEAD), 0)).astype(BF16)
     valid_len = len_ref[lax.axis_index(AXIS)]
@@ -95,9 +98,10 @@
         ones = jnp.broadcast_to(jnp.where(valid, 1.0, 0.0), (VROWS - HEAD, CHUNK))
         o_ref[HEAD:, span] = ones.astype(BF16)
     copies[-1].wait()
-
-
-def turned_values(lengths, keys, values):
+    blank.wait()
+
+
+def turned_values(lengths, keys, values, shape):
     count = values.shape[0]
     hbm_spec = pl.BlockSpec(memory_space=pltpu.HBM)
     vmem_spec = pl.BlockSpec(memory_space=pltpu.VMEM)
@@ -106,12 +110,14 @@
         out_shape=(
             jax.ShapeDtypeStruct((CHUNK, HEAD), BF16),
             jax.ShapeDtypeStruct((VROWS, count), BF16),
+            jax.ShapeDtypeStruct(shape, BF16),
         ),
         in_specs=[pl.BlockSpec(memory_space=pltpu.SMEM), hbm_spec, hbm_spec],
-        out_specs=(vmem_spec, vmem_spec),
+        out_specs=(vmem_spec, vmem_spec, hbm_spec),
         scratch_shapes=[
             pltpu.VMEM(values.shape, BF16),
-            pltpu.SemaphoreType.DMA((count // CHUNK + 1,)),
+            pltpu.VMEM(shape, BF16),
+            pltpu.SemaphoreType.DMA((count // CHUNK + 2,)),
         ],
         compiler_params=vmem(16),
         cost_estimate=pl.CostEstimate(
@@ -171,7 +177,8 @@
 
 
 def first_attention_kernel(q_ref, head_ref, k_ref, v_ref, o_ref, kept_ref, acc_ref, sems):
-    spans = [slice(start, start + CHUNK) for start in range(0, k_ref.shape[0], CHUNK)]
+    stops = [0, CHUNK, 2 * CHUNK, k_ref.shape[0]]
+    spans = [slice(*ends) for ends in zip(stops, stops[1:])]
     copies = [
         pltpu.make_async_copy(k_ref.at[span] if i else head_ref, kept_ref.at[span], sems.at[i])
         for i, span in enumerate(spans)
@@ -199,7 +206,7 @@
         out_specs=(vmem_spec, vmem_spec),
         scratch_shapes=[
             pltpu.VMEM((VROWS, BLOCK), F32),
-            pltpu.SemaphoreType.DMA((keys.shape[0] // CHUNK,)),
+            pltpu.SemaphoreType.DMA((3,)),
         ],
         compiler_params=vmem(44),
         cost_estimate=pl.CostEstimate(
@@ -327,15 +334,9 @@
     )(received)
 
 
-def place_kernel(owner_ref, a_ref, b_ref, o_ref):
-    half = o_ref.shape[1] // 2
-
+def place_kernel(owner_ref, own_ref, peer_ref, blank_ref, o_ref, held_ref, sem):
+    half = held_ref.shape[1] // 2
     me = lax.axis_index(AXIS)
-    wanted = me == owner_ref[0]
-
-    @pl.when(jnp.logical_not(wanted))
-    def _():
-        o_ref[...] = jnp.zeros_like(o_ref)
 
     def put(*halves):
         for core, ref in enumerate(halves):
@@ -344,36 +345,42 @@
                 for spot in range(0, PIECES, 2):
                     pieces = [ref[snake(chip)] for chip in chips[spot : spot + 2]]
                     column = core * half + (team * PIECES + spot) // 2 * HEAD
-                    o_ref[:, column : column + HEAD] = jnp.concatenate(pieces, axis=0).T
-
-    @pl.when(wanted & (me % 2 == 0))
+                    held_ref[:, column : column + HEAD] = jnp.concatenate(pieces, axis=0).T
+        copy = pltpu.make_async_copy(held_ref, o_ref, sem)
+        copy.start()
+        copy.wait()
+
+    @pl.when((me == owner_ref[0]) & (me % 2 == 0))
     def _():
-        put(a_ref, b_ref)
-
-    @pl.when(wanted & (me % 2 == 1))
+        put(own_ref, peer_ref)
+
+    @pl.when((me == owner_ref[0]) & (me % 2 == 1))
     def _():
-        put(b_ref, a_ref)
-
-
-def place(owner, own, other):
+        put(peer_ref, own_ref)
+
+
+def place(owner, own, peer, blank):
+    vmem_spec = pl.BlockSpec(memory_space=pltpu.VMEM)
+    hbm_spec = pl.BlockSpec(memory_space=pltpu.HBM)
     return pl.pallas_call(
         place_kernel,
-        out_shape=jax.ShapeDtypeStruct((HEAD, 2 * CHIPS * PIECE), BF16),
-        in_specs=[
-            pl.BlockSpec(memory_space=pltpu.SMEM),
-            pl.BlockSpec(memory_space=pltpu.VMEM),
-            pl.BlockSpec(memory_space=pltpu.VMEM),
-        ],
+        out_shape=jax.ShapeDtypeStruct(blank.shape, BF16),
+        in_specs=[pl.BlockSpec(memory_space=pltpu.SMEM), vmem_spec, vmem_spec, hbm_spec],
+        out_specs=hbm_spec,
+        scratch_shapes=[pltpu.VMEM(blank.shape, BF16), pltpu.SemaphoreType.DMA],
+        input_output_aliases={3: 0},
         compiler_params=vmem(16),
         name="place",
-    )(owner, own, other)
+    )(owner, own, peer, blank)
 
 
 def per_device(queries, cache_keys, cache_values, lengths, span_owner):
     keep, send = split(queries[0])
     mine = choose(span_owner, keep, lax.ppermute(send, AXIS, SWAP))
     lengths, mine = lax.optimization_barrier((lengths, mine))
-    first_keys, values = turned_values(lengths, cache_keys, cache_values)
+    first_keys, values, blank = turned_values(
+        lengths, cache_keys, cache_values, queries.shape[1:]
+    )
     y, x = span_owner[0] // (2 * COLUMNS), span_owner[0] // 2 % COLUMNS
     slot = y * COLUMNS + jnp.where(y % 2 == 1, COLUMNS - 1 - x, x)
     piece = lax.dynamic_index_in_dim(exchange(mine, PLANE), slot, 0, False)
@@ -399,7 +406,7 @@
 
     received = exchange(merge(part, peer_here, merge(here)), TEAMS)
     result = exchange(finish(received), PLANE)
-    out = place(span_owner, result, lax.ppermute(result, AXIS, SWAP))
+    out = place(span_owner, result, lax.ppermute(result, AXIS, SWAP), blank)
     return out[None]
 
 

time: 106 us -> 106 us (level)
  transfers between devices with their start and end apart: 9 -> 9, of which waited for: 4 -> 4; matrix products, arithmetic and copies ran while one was open for 0% -> 0% of each run, Pallas kernels for 27% -> 28%
where the time goes in v5:
time: 106 us; the launch traced here: 105 us
  starting transfers between devices  37.5 us (35%)
  Pallas kernels  31.2 us (29%)
  blocking collectives  29.6 us (28%)
  waiting for transfers between devices  5.14 us (5%)
  between operations  1.06 us (1%)
    all_to_all x3, blocking collectives, exchange(): lax.all_to_all(pieces, AXIS, 0, 0, axis_index_groups=groups, tiled=True)  29.6 us
    pallas_call x3, Pallas kernels, attention(): pl.pallas_call(attention_kernel, out_shape=jax.ShapeDtypeStruct((PIECES,...  21.6 us
    ppermute x1, starting transfers between devices, per_device(): here = lax.ppermute(away, AXIS, CROSS)  12.2 us
    ppermute x1, starting transfers between devices, per_device(): out = place(span_owner, result, lax.ppermute(result, AXIS, SWAP), blank)  11.9 us
    all_to_all x1, starting transfers between devices, exchange(): lax.all_to_all(pieces, AXIS, 0, 0, axis_index_groups=groups, tiled=True)  5.02 us
    pallas_call x1, Pallas kernels, first_attention(): pl.pallas_call(first_attention_kernel, out_shape=(jax.ShapeDtypeStruct((P...  4.31 us
    ppermute x1, starting transfers between devices, per_device(): mine = choose(span_owner, keep, lax.ppermute(send, AXIS, SWAP))  3.33 us
    all_to_all x1, waiting for transfers between devices, exchange(): lax.all_to_all(pieces, AXIS, 0, 0, axis_index_groups=groups, tiled=True)  3.29 us
  transfers between devices with their start and end apart: 9, of which 4 were waited for; matrix products, arithmetic and copies ran while one was open for 0% of the time, Pallas kernels for 28%

profile of v5, /device:TPU:1, one launch (start us, length us, event | category | flops | bytes accessed | tf_op | source)
XLA Modules:
  0.0 105.1 jit_solution(378061925016318620)
XLA Ops:
  0.0 1.3 %split.1 = (bf16[16,64,128]{2,1,0:T(8,128)(2,1)S(1)}, bf16[16,64,128]{2,1,0:T(8,128)(2,1)S(1)}) custom-call(bf16[128,2048]{1,0:T(8,128)(2,1)} %bitcast.17), custom_call_target="tpu_custom_call" | custom-call | tf_op jit(solution)/shard_map/split/pallas_call | solution.py:282
  1.3 3.3 %collective-permute-start = (bf16[16,64,128]{2,1,0:T(8,128)(2,1)S(1)}, bf16[16,64,128]{2,1,0:T(8,128)(2,1)S(1)}, u32[]{:S(2)}, u32[]{:S(2)}) collective-permute-start(bf16[16,64,128]{2,1,0:T(8,128)(2,1)S(1)} %get-tuple-element.24), channel_id=1, source_target_pairs={{0,8},{8,0},{16,24},{24,16},{32,40},{40,32},{48,56},{56,48},{64,72... | collective-permute-start | bytes 786440 | tf_op jit(solution)/shard_map/ppermute | solution.py:379
  5.3 0.5 collective-permute-done.b_ref
  5.8 0.7 choose.1
  6.5 5.0 %all-to-all-start = ((bf16[16,64,128]{2,1,0:T(8,128)(2,1)}), bf16[16,64,128]{2,1,0:T(8,128)(2,1)S(1)}, u32[]{:S(2)}, u32[]{:S(2)}) async-start(bf16[16,64,128]{2,1,0:T(8,128)(2,1)} %choose.1), calls=%async_computation | async-start | bytes 524288 | tf_op jit(solution)/shard_map/all_to_all | solution.py:71
  11.6 0.6 copy-done
  12.3 3.0 %turn_values.1 = (bf16[2048,128]{1,0:T(8,128)(2,1)S(1)}, bf16[144,8192]{1,0:T(8,128)(2,1)S(1)}, bf16[128,2048]{1,0:T(8,128)(2,1)}) custom-call(s32[32]{0:T(128)S(1)} %copy-done, bf16[8192,128]{1,0:T(8,128)(2,1)} %k_ref.3, bf16[8192,128]{1,0:T(8,128)(2,1)} %v_ref.1), custom_call_target="tpu_custom_call" | custom-call | flops 536870912 | bytes 5242880 | tf_op jit(solution)/shard_map/turn_values/pallas_call | solution.py:108
  15.3 3.3 %all-to-all-done = bf16[16,64,128]{2,1,0:T(8,128)(2,1)S(1)} async-done(((bf16[16,64,128]{2,1,0:T(8,128)(2,1)}), bf16[16,64,128]{2,1,0:T(8,128)(2,1)S(1)}, u32[]{:S(2)}, u32[]{:S(2)}) %all-to-all-start) | async-done | bytes 262176 | tf_op jit(solution)/shard_map/all_to_all | solution.py:71
  18.6 8.2 %all_to_all.20 = bf16[8,64,128]{2,1,0:T(8,128)(2,1)S(1)} all-to-all(bf16[8,64,128]{2,1,0:T(8,128)(2,1)S(1)} %broadcast_in_dim.4), channel_id=1, replica_groups={{0,64,16,80,32,96,48,112},{128,192,144,208,160,224,176,240},{8,24,72,88..., dimensions={0} | all-to-all | bytes 262144 | tf_op jit(solution)/shard_map/all_to_all | solution.py:71
  26.8 2.9 %collective-permute-start.1 = (bf16[8,64,128]{2,1,0:T(8,128)(2,1)S(1)}, bf16[8,64,128]{2,1,0:T(8,128)(2,1)S(1)}, u32[]{:S(2)}, u32[]{:S(2)}) collective-permute-start(bf16[8,64,128]{2,1,0:T(8,128)(2,1)S(1)} %all_to_all.20), channel_id=1, source_target_pairs={{0,8},{8,0},{16,24},{24,16},{32,40},{40,32},{48,56},{56,48},{64,72... | collective-permute-start | bytes 393224 | tf_op jit(solution)/shard_map/ppermute | solution.py:390
  29.8 0.8 collective-permute-start.2
  30.6 4.3 %first_attention.1 = (f32[8,72,128]{2,1,0:T(8,128)S(1)}, bf16[8192,128]{1,0:T(8,128)(2,1)S(1)}) custom-call(bf16[512,128]{1,0:T(8,128)(2,1)S(1)} %bitcast.13, bf16[2048,128]{1,0:T(8,128)(2,1)S(1)} %get-tuple-element.30.head_ref, bf16[8192,128]{1,0:T(8,128)(2,1)} %k_ref.3, bf16[144,8192]{1,0:T(8,128)(2,1)S(1)} %get-tuple-element.31.v_ref), custom_call_target="tpu_custom_call" | custom-call | flops 268435456 | bytes 1048576 | tf_op jit(solution)/shard_map/first_attention/pallas_call | solution.py:199
  34.9 0.2 collective-permute-done.2
  35.1 0.9 collective-permute-start.3
  36.0 0.2 collective-permute-start.4
  36.1 3.7 %attention.3.refs_0_ = f32[8,72,128]{2,1,0:T(8,128)S(1)} custom-call(bf16[512,128]{1,0:T(8,128)(2,1)S(1)} %bitcast.15, bf16[8192,128]{1,0:T(8,128)(2,1)S(1)} %get-tuple-element.34.k_ref, bf16[144,8192]{1,0:T(8,128)(2,1)S(1)} %get-tuple-element.31.v_ref), custom_call_target="tpu_custom_call" | custom-call | flops 268435456 | bytes 1048576 | tf_op jit(solution)/shard_map/attention/pallas_call | solution.py:221
  39.9 12.2 %collective-permute-start.6 = (f32[8,72,128]{2,1,0:T(8,128)S(1)}, f32[8,72,128]{2,1,0:T(8,128)S(1)}, u32[]{:S(2)}, u32[]{:S(2)}) collective-permute-start(f32[8,72,128]{2,1,0:T(8,128)S(1)} %merge.3), channel_id=1, source_target_pairs={{8,192},{0,56},{24,208},{16,40},{40,224},{32,24},{56,240},{48,8},{... | collective-permute-start | bytes 884744 | tf_op jit(solution)/shard_map/ppermute | solution.py:401
  52.0 14.3 %attention.4 = f32[8,72,128]{2,1,0:T(8,128)S(1)} custom-call(bf16[512,128]{1,0:T(8,128)(2,1)S(1)} %bitcast.16, bf16[8192,128]{1,0:T(8,128)(2,1)S(1)} %get-tuple-element.34.k_ref, bf16[144,8192]{1,0:T(8,128)(2,1)S(1)} %get-tuple-element.31.v_ref), custom_call_target="tpu_custom_call" | custom-call | flops 268435456 | bytes 1048576 | tf_op jit(solution)/shard_map/attention/pallas_call | solution.py:221
  66.3 0.3 collective-permute-start.5
  66.7 3.7 %attention.5.refs_0_ = f32[8,72,128]{2,1,0:T(8,128)S(1)} custom-call(bf16[512,128]{1,0:T(8,128)(2,1)S(1)} %bitcast.14, bf16[8192,128]{1,0:T(8,128)(2,1)S(1)} %get-tuple-element.34.k_ref, bf16[144,8192]{1,0:T(8,128)(2,1)S(1)} %get-tuple-element.31.v_ref), custom_call_target="tpu_custom_call" | custom-call | flops 268435456 | bytes 1048576 | tf_op jit(solution)/shard_map/attention/pallas_call | solution.py:221
  70.5 9.8 %all_to_all.21.r_ref = f32[8,72,128]{2,1,0:T(8,128)S(1)} all-to-all(f32[8,72,128]{2,1,0:T(8,128)S(1)} %merge.5), channel_id=1, replica_groups={{0,64,16,80,32,96,48,112},{128,192,144,208,160,224,176,240},{8,24,72,88..., dimensions={0} | all-to-all | bytes 589824 | tf_op jit(solution)/shard_map/all_to_all | solution.py:71
  80.4 11.6 %all_to_all.22.own_ref = bf16[16,64,128]{2,1,0:T(8,128)(2,1)S(1)} all-to-all(bf16[16,64,128]{2,1,0:T(8,128)(2,1)S(1)} %finish.1), channel_id=1, replica_groups={{0,16,32,48,112,96,80,64,128,144,160,176,240,224,208,192},{8,24,40,56,1..., dimensions={0} | all-to-all | bytes 524288 | tf_op jit(solution)/shard_map/all_to_all | solution.py:71
  91.9 11.9 %collective-permute-start.7 = (bf16[16,64,128]{2,1,0:T(8,128)(2,1)S(1)}, bf16[16,64,128]{2,1,0:T(8,128)(2,1)S(1)}, u32[]{:S(2)}, u32[]{:S(2)}) collective-permute-start(bf16[16,64,128]{2,1,0:T(8,128)(2,1)S(1)} %all_to_all.22.own_ref), channel_id=1, source_target_pairs={{0,8},{8,0},{16,24},{24,16},{32,40},{40,32},{48,56},{56,48},{64,72... | collective-permute-start | bytes 786440 | tf_op jit(solution)/shard_map/ppermute | solution.py:409
  103.8 1.2 %collective-permute-done.7.peer_ref = bf16[16,64,128]{2,1,0:T(8,128)(2,1)S(1)} collective-permute-done((bf16[16,64,128]{2,1,0:T(8,128)(2,1)S(1)}, bf16[16,64,128]{2,1,0:T(8,128)(2,1)S(1)}, u32[]{:S(2)}, u32[]{:S(2)}) %collective-permute-start.7) | collective-permute-done | bytes 262176 | tf_op jit(solution)/shard_map/ppermute | solution.py:409
  (13 shorter events, 0.3 us)
Async XLA Ops:
  1.3 4.5 %collective-permute-start = (bf16[16,64,128]{2,1,0:T(8,128)(2,1)S(1)}, bf16[16,64,128]{2,1,0:T(8,128)(2,1)S(1)}, u32[]{:S(2)}, u32[]{:S(2)}) collective-permute-start(bf16[16,64,128]{2,1,0:T(8,128)(2,1)S(1)} %get-tuple-element.24), channel_id=1, source_target_pairs={{0,8},{8,0},{16,24},{24,16},{32,40},{40,32},{48,56},{56,48},{64,72... | collective-permute-start | bytes 786440 | tf_op jit(solution)/shard_map/ppermute | solution.py:379
  6.5 12.1 %all-to-all-start = ((bf16[16,64,128]{2,1,0:T(8,128)(2,1)}), bf16[16,64,128]{2,1,0:T(8,128)(2,1)S(1)}, u32[]{:S(2)}, u32[]{:S(2)}) async-start(bf16[16,64,128]{2,1,0:T(8,128)(2,1)} %choose.1), calls=%async_computation | async-start | bytes 524288 | tf_op jit(solution)/shard_map/all_to_all | solution.py:71
  11.6 0.7 copy-start
  26.8 8.1 %collective-permute-start.1 = (bf16[8,64,128]{2,1,0:T(8,128)(2,1)S(1)}, bf16[8,64,128]{2,1,0:T(8,128)(2,1)S(1)}, u32[]{:S(2)}, u32[]{:S(2)}) collective-permute-start(bf16[8,64,128]{2,1,0:T(8,128)(2,1)S(1)} %all_to_all.20), channel_id=1, source_target_pairs={{0,8},{8,0},{16,24},{24,16},{32,40},{40,32},{48,56},{56,48},{64,72... | collective-permute-start | bytes 393224 | tf_op jit(solution)/shard_map/ppermute | solution.py:390
  29.8 5.3 %collective-permute-start.2 = (bf16[8,64,128]{2,1,0:T(8,128)(2,1)S(1)}, bf16[8,64,128]{2,1,0:T(8,128)(2,1)S(1)}, u32[]{:S(2)}, u32[]{:S(2)}) collective-permute-start(bf16[8,64,128]{2,1,0:T(8,128)(2,1)S(1)} %all_to_all.20), channel_id=1, source_target_pairs={{0,192},{8,56},{16,208},{24,40},{32,224},{40,24},{48,240},{56,8},{... | collective-permute-start | bytes 393224 | tf_op jit(solution)/shard_map/ppermute | solution.py:391
  35.1 4.7 %collective-permute-start.3 = (f32[8,72,128]{2,1,0:T(8,128)S(1)}, f32[8,72,128]{2,1,0:T(8,128)S(1)}, u32[]{:S(2)}, u32[]{:S(2)}) collective-permute-start(f32[8,72,128]{2,1,0:T(8,128)S(1)} %get-tuple-element.35), channel_id=1, source_target_pairs={{0,8},{8,0},{16,24},{24,16},{32,40},{40,32},{48,56},{56,48},{64,72... | collective-permute-start | bytes 884744 | tf_op jit(solution)/shard_map/ppermute | solution.py:396
  36.0 3.9 %collective-permute-start.4 = (bf16[8,64,128]{2,1,0:T(8,128)(2,1)S(1)}, bf16[8,64,128]{2,1,0:T(8,128)(2,1)S(1)}, u32[]{:S(2)}, u32[]{:S(2)}) collective-permute-start(bf16[8,64,128]{2,1,0:T(8,128)(2,1)S(1)} %collective-permute-done.2), channel_id=1, source_target_pairs={{0,8},{8,0},{16,24},{24,16},{32,40},{40,32},{48,56},{56,48},{64,72... | collective-permute-start | bytes 393224 | tf_op jit(solution)/shard_map/ppermute | solution.py:397
  39.9 30.5 %collective-permute-start.6 = (f32[8,72,128]{2,1,0:T(8,128)S(1)}, f32[8,72,128]{2,1,0:T(8,128)S(1)}, u32[]{:S(2)}, u32[]{:S(2)}) collective-permute-start(f32[8,72,128]{2,1,0:T(8,128)S(1)} %merge.3), channel_id=1, source_target_pairs={{8,192},{0,56},{24,208},{16,40},{40,224},{32,24},{56,240},{48,8},{... | collective-permute-start | bytes 884744 | tf_op jit(solution)/shard_map/ppermute | solution.py:401
  66.3 4.1 %collective-permute-start.5 = (f32[8,72,128]{2,1,0:T(8,128)S(1)}, f32[8,72,128]{2,1,0:T(8,128)S(1)}, u32[]{:S(2)}, u32[]{:S(2)}) collective-permute-start(f32[8,72,128]{2,1,0:T(8,128)S(1)} %attention.4), channel_id=1, source_target_pairs={{0,8},{8,0},{16,24},{24,16},{32,40},{40,32},{48,56},{56,48},{64,72... | collective-permute-start | bytes 884744 | tf_op jit(solution)/shard_map/ppermute | solution.py:403
  91.9 13.0 %collective-permute-start.7 = (bf16[16,64,128]{2,1,0:T(8,128)(2,1)S(1)}, bf16[16,64,128]{2,1,0:T(8,128)(2,1)S(1)}, u32[]{:S(2)}, u32[]{:S(2)}) collective-permute-start(bf16[16,64,128]{2,1,0:T(8,128)(2,1)S(1)} %all_to_all.22.own_ref), channel_id=1, source_target_pairs={{0,8},{8,0},{16,24},{24,16},{32,40},{40,32},{48,56},{56,48},{64,72... | collective-permute-start | bytes 786440 | tf_op jit(solution)/shard_map/ppermute | solution.py:409

commit v6 on v5

--- a/solution.py
+++ b/solution.py
@@ -290,27 +290,31 @@
     )(in_hbm(block))
 
 
-def choose_kernel(owner_ref, a_ref, b_ref, o_ref):
+def choose_kernel(owner_ref, a_ref, b_ref, o_ref, sem):
     mine = owner_ref[0] % 2 == lax.axis_index(AXIS) % 2
+
+    def put(ref):
+        copy = pltpu.make_async_copy(ref, o_ref, sem)
+        copy.start()
+        copy.wait()
 
     @pl.when(mine)
     def _():
-        o_ref[...] = a_ref[...]
+        put(a_ref)
 
     @pl.when(jnp.logical_not(mine))
     def _():
-        o_ref[...] = b_ref[...]
+        put(b_ref)
 
 
 def choose(owner, a, b):
+    vmem_spec = pl.BlockSpec(memory_space=pltpu.VMEM)
     return pl.pallas_call(
         choose_kernel,
         out_shape=jax.ShapeDtypeStruct(a.shape, a.dtype),
-        in_specs=[
-            pl.BlockSpec(memory_space=pltpu.SMEM),
-            pl.BlockSpec(memory_space=pltpu.VMEM),
-            pl.BlockSpec(memory_space=pltpu.VMEM),
-        ],
+        in_specs=[pl.BlockSpec(memory_space=pltpu.SMEM), vmem_spec, vmem_spec],
+        out_specs=pl.BlockSpec(memory_space=pltpu.HBM),
+        scratch_shapes=[pltpu.SemaphoreType.DMA],
         compiler_params=vmem(16),
         name="choose",
     )(owner, a, b)

time: 106 us -> 106 us (level)
  no operation moved by 1% of the time
where the time goes in v6:
time: 106 us; the launch traced here: 105 us
  starting transfers between devices  37.5 us (35%)
  Pallas kernels  31.2 us (29%)
  blocking collectives  29.6 us (28%)
  waiting for transfers between devices  5.13 us (5%)
  between operations  1.07 us (1%)
    all_to_all x3, blocking collectives, exchange(): lax.all_to_all(pieces, AXIS, 0, 0, axis_index_groups=groups, tiled=True)  29.6 us
    pallas_call x3, Pallas kernels, attention(): pl.pallas_call(attention_kernel, out_shape=jax.ShapeDtypeStruct((PIECES,...  21.6 us
    ppermute x1, starting transfers between devices, per_device(): here = lax.ppermute(away, AXIS, CROSS)  12.2 us
    ppermute x1, starting transfers between devices, per_device(): out = place(span_owner, result, lax.ppermute(result, AXIS, SWAP), blank)  11.9 us
    all_to_all x1, starting transfers between devices, exchange(): lax.all_to_all(pieces, AXIS, 0, 0, axis_index_groups=groups, tiled=True)  5.03 us
    pallas_call x1, Pallas kernels, first_attention(): pl.pallas_call(first_attention_kernel, out_shape=(jax.ShapeDtypeStruct((P...  4.32 us
    ppermute x1, starting transfers between devices, per_device(): mine = choose(span_owner, keep, lax.ppermute(send, AXIS, SWAP))  3.33 us
    all_to_all x1, waiting for transfers between devices, exchange(): lax.all_to_all(pieces, AXIS, 0, 0, axis_index_groups=groups, tiled=True)  3.29 us
  transfers between devices with their start and end apart: 9, of which 4 were waited for; matrix products, arithmetic and copies ran while one was open for 0% of the time, Pallas kernels for 28%

profile of v6, /device:TPU:1, one launch (start us, length us, event | category | flops | bytes accessed | tf_op | source)
XLA Modules:
  0.0 105.2 jit_solution(12554440191783091408)
XLA Ops:
  0.0 1.3 %split.1 = (bf16[16,64,128]{2,1,0:T(8,128)(2,1)S(1)}, bf16[16,64,128]{2,1,0:T(8,128)(2,1)S(1)}) custom-call(bf16[128,2048]{1,0:T(8,128)(2,1)} %bitcast.17), custom_call_target="tpu_custom_call" | custom-call | tf_op jit(solution)/shard_map/split/pallas_call | solution.py:282
  1.3 3.3 %collective-permute-start = (bf16[16,64,128]{2,1,0:T(8,128)(2,1)S(1)}, bf16[16,64,128]{2,1,0:T(8,128)(2,1)S(1)}, u32[]{:S(2)}, u32[]{:S(2)}) collective-permute-start(bf16[16,64,128]{2,1,0:T(8,128)(2,1)S(1)} %get-tuple-element.24), channel_id=1, source_target_pairs={{0,8},{8,0},{16,24},{24,16},{32,40},{40,32},{48,56},{56,48},{64,72... | collective-permute-start | bytes 786440 | tf_op jit(solution)/shard_map/ppermute | solution.py:383
  5.3 0.5 collective-permute-done.b_ref
  5.8 0.7 choose.1
  6.5 5.0 %all-to-all-start = ((bf16[16,64,128]{2,1,0:T(8,128)(2,1)}), bf16[16,64,128]{2,1,0:T(8,128)(2,1)S(1)}, u32[]{:S(2)}, u32[]{:S(2)}) async-start(bf16[16,64,128]{2,1,0:T(8,128)(2,1)} %choose.1), calls=%async_computation | async-start | bytes 524288 | tf_op jit(solution)/shard_map/all_to_all | solution.py:71
  11.6 0.6 copy-done
  12.3 3.0 %turn_values.1 = (bf16[2048,128]{1,0:T(8,128)(2,1)S(1)}, bf16[144,8192]{1,0:T(8,128)(2,1)S(1)}, bf16[128,2048]{1,0:T(8,128)(2,1)}) custom-call(s32[32]{0:T(128)S(1)} %copy-done, bf16[8192,128]{1,0:T(8,128)(2,1)} %k_ref.3, bf16[8192,128]{1,0:T(8,128)(2,1)} %v_ref.1), custom_call_target="tpu_custom_call" | custom-call | flops 536870912 | bytes 5242880 | tf_op jit(solution)/shard_map/turn_values/pallas_call | solution.py:108
  15.3 3.3 %all-to-all-done = bf16[16,64,128]{2,1,0:T(8,128)(2,1)S(1)} async-done(((bf16[16,64,128]{2,1,0:T(8,128)(2,1)}), bf16[16,64,128]{2,1,0:T(8,128)(2,1)S(1)}, u32[]{:S(2)}, u32[]{:S(2)}) %all-to-all-start) | async-done | bytes 262176 | tf_op jit(solution)/shard_map/all_to_all | solution.py:71
  18.6 8.2 %all_to_all.20 = bf16[8,64,128]{2,1,0:T(8,128)(2,1)S(1)} all-to-all(bf16[8,64,128]{2,1,0:T(8,128)(2,1)S(1)} %broadcast_in_dim.4), channel_id=1, replica_groups={{0,64,16,80,32,96,48,112},{128,192,144,208,160,224,176,240},{8,24,72,88..., dimensions={0} | all-to-all | bytes 262144 | tf_op jit(solution)/shard_map/all_to_all | solution.py:71
  26.8 2.9 %collective-permute-start.1 = (bf16[8,64,128]{2,1,0:T(8,128)(2,1)S(1)}, bf16[8,64,128]{2,1,0:T(8,128)(2,1)S(1)}, u32[]{:S(2)}, u32[]{:S(2)}) collective-permute-start(bf16[8,64,128]{2,1,0:T(8,128)(2,1)S(1)} %all_to_all.20), channel_id=1, source_target_pairs={{0,8},{8,0},{16,24},{24,16},{32,40},{40,32},{48,56},{56,48},{64,72... | collective-permute-start | bytes 393224 | tf_op jit(solution)/shard_map/ppermute | solution.py:394
  29.8 0.8 collective-permute-start.2
  30.6 4.3 %first_attention.1 = (f32[8,72,128]{2,1,0:T(8,128)S(1)}, bf16[8192,128]{1,0:T(8,128)(2,1)S(1)}) custom-call(bf16[512,128]{1,0:T(8,128)(2,1)S(1)} %bitcast.13, bf16[2048,128]{1,0:T(8,128)(2,1)S(1)} %get-tuple-element.30.head_ref, bf16[8192,128]{1,0:T(8,128)(2,1)} %k_ref.3, bf16[144,8192]{1,0:T(8,128)(2,1)S(1)} %get-tuple-element.31.v_ref), custom_call_target="tpu_custom_call" | custom-call | flops 268435456 | bytes 1048576 | tf_op jit(solution)/shard_map/first_attention/pallas_call | solution.py:199
  35.0 0.2 collective-permute-done.2
  35.1 0.9 collective-permute-start.3
  36.0 0.2 collective-permute-start.4
  36.1 3.7 %attention.3.refs_0_ = f32[8,72,128]{2,1,0:T(8,128)S(1)} custom-call(bf16[512,128]{1,0:T(8,128)(2,1)S(1)} %bitcast.15, bf16[8192,128]{1,0:T(8,128)(2,1)S(1)} %get-tuple-element.34.k_ref, bf16[144,8192]{1,0:T(8,128)(2,1)S(1)} %get-tuple-element.31.v_ref), custom_call_target="tpu_custom_call" | custom-call | flops 268435456 | bytes 1048576 | tf_op jit(solution)/shard_map/attention/pallas_call | solution.py:221
  39.9 12.2 %collective-permute-start.6 = (f32[8,72,128]{2,1,0:T(8,128)S(1)}, f32[8,72,128]{2,1,0:T(8,128)S(1)}, u32[]{:S(2)}, u32[]{:S(2)}) collective-permute-start(f32[8,72,128]{2,1,0:T(8,128)S(1)} %merge.3), channel_id=1, source_target_pairs={{8,192},{0,56},{24,208},{16,40},{40,224},{32,24},{56,240},{48,8},{... | collective-permute-start | bytes 884744 | tf_op jit(solution)/shard_map/ppermute | solution.py:405
  52.1 14.3 %attention.4 = f32[8,72,128]{2,1,0:T(8,128)S(1)} custom-call(bf16[512,128]{1,0:T(8,128)(2,1)S(1)} %bitcast.16, bf16[8192,128]{1,0:T(8,128)(2,1)S(1)} %get-tuple-element.34.k_ref, bf16[144,8192]{1,0:T(8,128)(2,1)S(1)} %get-tuple-element.31.v_ref), custom_call_target="tpu_custom_call" | custom-call | flops 268435456 | bytes 1048576 | tf_op jit(solution)/shard_map/attention/pallas_call | solution.py:221
  66.3 0.3 collective-permute-start.5
  66.7 3.7 %attention.5.refs_0_ = f32[8,72,128]{2,1,0:T(8,128)S(1)} custom-call(bf16[512,128]{1,0:T(8,128)(2,1)S(1)} %bitcast.14, bf16[8192,128]{1,0:T(8,128)(2,1)S(1)} %get-tuple-element.34.k_ref, bf16[144,8192]{1,0:T(8,128)(2,1)S(1)} %get-tuple-element.31.v_ref), custom_call_target="tpu_custom_call" | custom-call | flops 268435456 | bytes 1048576 | tf_op jit(solution)/shard_map/attention/pallas_call | solution.py:221
  70.5 9.8 %all_to_all.21.r_ref = f32[8,72,128]{2,1,0:T(8,128)S(1)} all-to-all(f32[8,72,128]{2,1,0:T(8,128)S(1)} %merge.5), channel_id=1, replica_groups={{0,64,16,80,32,96,48,112},{128,192,144,208,160,224,176,240},{8,24,72,88..., dimensions={0} | all-to-all | bytes 589824 | tf_op jit(solution)/shard_map/all_to_all | solution.py:71
  80.4 11.6 %all_to_all.22.own_ref = bf16[16,64,128]{2,1,0:T(8,128)(2,1)S(1)} all-to-all(bf16[16,64,128]{2,1,0:T(8,128)(2,1)S(1)} %finish.1), channel_id=1, replica_groups={{0,16,32,48,112,96,80,64,128,144,160,176,240,224,208,192},{8,24,40,56,1..., dimensions={0} | all-to-all | bytes 524288 | tf_op jit(solution)/shard_map/all_to_all | solution.py:71
  92.0 11.9 %collective-permute-start.7 = (bf16[16,64,128]{2,1,0:T(8,128)(2,1)S(1)}, bf16[16,64,128]{2,1,0:T(8,128)(2,1)S(1)}, u32[]{:S(2)}, u32[]{:S(2)}) collective-permute-start(bf16[16,64,128]{2,1,0:T(8,128)(2,1)S(1)} %all_to_all.22.own_ref), channel_id=1, source_target_pairs={{0,8},{8,0},{16,24},{24,16},{32,40},{40,32},{48,56},{56,48},{64,72... | collective-permute-start | bytes 786440 | tf_op jit(solution)/shard_map/ppermute | solution.py:413
  103.8 1.2 %collective-permute-done.7.peer_ref = bf16[16,64,128]{2,1,0:T(8,128)(2,1)S(1)} collective-permute-done((bf16[16,64,128]{2,1,0:T(8,128)(2,1)S(1)}, bf16[16,64,128]{2,1,0:T(8,128)(2,1)S(1)}, u32[]{:S(2)}, u32[]{:S(2)}) %collective-permute-start.7) | collective-permute-done | bytes 262176 | tf_op jit(solution)/shard_map/ppermute | solution.py:413
  (13 shorter events, 0.3 us)
Async XLA Ops:
  1.3 4.5 %collective-permute-start = (bf16[16,64,128]{2,1,0:T(8,128)(2,1)S(1)}, bf16[16,64,128]{2,1,0:T(8,128)(2,1)S(1)}, u32[]{:S(2)}, u32[]{:S(2)}) collective-permute-start(bf16[16,64,128]{2,1,0:T(8,128)(2,1)S(1)} %get-tuple-element.24), channel_id=1, source_target_pairs={{0,8},{8,0},{16,24},{24,16},{32,40},{40,32},{48,56},{56,48},{64,72... | collective-permute-start | bytes 786440 | tf_op jit(solution)/shard_map/ppermute | solution.py:383
  6.5 12.1 %all-to-all-start = ((bf16[16,64,128]{2,1,0:T(8,128)(2,1)}), bf16[16,64,128]{2,1,0:T(8,128)(2,1)S(1)}, u32[]{:S(2)}, u32[]{:S(2)}) async-start(bf16[16,64,128]{2,1,0:T(8,128)(2,1)} %choose.1), calls=%async_computation | async-start | bytes 524288 | tf_op jit(solution)/shard_map/all_to_all | solution.py:71
  11.6 0.7 copy-start
  26.8 8.1 %collective-permute-start.1 = (bf16[8,64,128]{2,1,0:T(8,128)(2,1)S(1)}, bf16[8,64,128]{2,1,0:T(8,128)(2,1)S(1)}, u32[]{:S(2)}, u32[]{:S(2)}) collective-permute-start(bf16[8,64,128]{2,1,0:T(8,128)(2,1)S(1)} %all_to_all.20), channel_id=1, source_target_pairs={{0,8},{8,0},{16,24},{24,16},{32,40},{40,32},{48,56},{56,48},{64,72... | collective-permute-start | bytes 393224 | tf_op jit(solution)/shard_map/ppermute | solution.py:394
  29.8 5.3 %collective-permute-start.2 = (bf16[8,64,128]{2,1,0:T(8,128)(2,1)S(1)}, bf16[8,64,128]{2,1,0:T(8,128)(2,1)S(1)}, u32[]{:S(2)}, u32[]{:S(2)}) collective-permute-start(bf16[8,64,128]{2,1,0:T(8,128)(2,1)S(1)} %all_to_all.20), channel_id=1, source_target_pairs={{0,192},{8,56},{16,208},{24,40},{32,224},{40,24},{48,240},{56,8},{... | collective-permute-start | bytes 393224 | tf_op jit(solution)/shard_map/ppermute | solution.py:395
  35.1 4.7 %collective-permute-start.3 = (f32[8,72,128]{2,1,0:T(8,128)S(1)}, f32[8,72,128]{2,1,0:T(8,128)S(1)}, u32[]{:S(2)}, u32[]{:S(2)}) collective-permute-start(f32[8,72,128]{2,1,0:T(8,128)S(1)} %get-tuple-element.35), channel_id=1, source_target_pairs={{0,8},{8,0},{16,24},{24,16},{32,40},{40,32},{48,56},{56,48},{64,72... | collective-permute-start | bytes 884744 | tf_op jit(solution)/shard_map/ppermute | solution.py:400
  36.0 3.9 %collective-permute-start.4 = (bf16[8,64,128]{2,1,0:T(8,128)(2,1)S(1)}, bf16[8,64,128]{2,1,0:T(8,128)(2,1)S(1)}, u32[]{:S(2)}, u32[]{:S(2)}) collective-permute-start(bf16[8,64,128]{2,1,0:T(8,128)(2,1)S(1)} %collective-permute-done.2), channel_id=1, source_target_pairs={{0,8},{8,0},{16,24},{24,16},{32,40},{40,32},{48,56},{56,48},{64,72... | collective-permute-start | bytes 393224 | tf_op jit(solution)/shard_map/ppermute | solution.py:401
  39.9 30.5 %collective-permute-start.6 = (f32[8,72,128]{2,1,0:T(8,128)S(1)}, f32[8,72,128]{2,1,0:T(8,128)S(1)}, u32[]{:S(2)}, u32[]{:S(2)}) collective-permute-start(f32[8,72,128]{2,1,0:T(8,128)S(1)} %merge.3), channel_id=1, source_target_pairs={{8,192},{0,56},{24,208},{16,40},{40,224},{32,24},{56,240},{48,8},{... | collective-permute-start | bytes 884744 | tf_op jit(solution)/shard_map/ppermute | solution.py:405
  66.3 4.1 %collective-permute-start.5 = (f32[8,72,128]{2,1,0:T(8,128)S(1)}, f32[8,72,128]{2,1,0:T(8,128)S(1)}, u32[]{:S(2)}, u32[]{:S(2)}) collective-permute-start(f32[8,72,128]{2,1,0:T(8,128)S(1)} %attention.4), channel_id=1, source_target_pairs={{0,8},{8,0},{16,24},{24,16},{32,40},{40,32},{48,56},{56,48},{64,72... | collective-permute-start | bytes 884744 | tf_op jit(solution)/shard_map/ppermute | solution.py:407
  92.0 13.0 %collective-permute-start.7 = (bf16[16,64,128]{2,1,0:T(8,128)(2,1)S(1)}, bf16[16,64,128]{2,1,0:T(8,128)(2,1)S(1)}, u32[]{:S(2)}, u32[]{:S(2)}) collective-permute-start(bf16[16,64,128]{2,1,0:T(8,128)(2,1)S(1)} %all_to_all.22.own_ref), channel_id=1, source_target_pairs={{0,8},{8,0},{16,24},{24,16},{32,40},{40,32},{48,56},{56,48},{64,72... | collective-permute-start | bytes 786440 | tf_op jit(solution)/shard_map/ppermute | solution.py:413
